TPU v7x, 256 devices: a whole 4x4x8 slice. The times are simulated.
256 devices in a mesh: row: 32 (over x, y, core), col: 8 (over z).
Axes of the slice: x: 4, y: 4, z: 8, core: 2. Of those that a mesh axis runs over, the one named last changes fastest.
Arguments:
- features: bfloat16 [65536, 256], P(('row', 'col')), may hold values from -6 to 6
- weight_one: bfloat16 [256, 256], replicated, may hold values from -0.375 to 0.375
- weight_two: bfloat16 [256, 172], replicated, may hold values from -0.375 to 0.375
- adj_tiles: bfloat16 [32, 8, 128, 128, 128], P('row', 'col'), may hold values from -0.109375 to 0.109375
- tile_rows: int32 [32, 8, 128], P('row', 'col'), may hold values from 0 to 15
- tile_cols: int32 [32, 8, 128], P('row', 'col'), may hold values from 0 to 63
- tile_counts: int32 [32, 8], P('row', 'col'), may hold values from 32 to 128, as said below
- labels: int32 [65536], P('row'), may hold values from 0 to 171
Outputs:
- logits: float32 [65536, 172], P(('row', 'col'))
- grad_one: float32 [256, 256], replicated
- grad_two: float32 [256, 172], replicated
Inputs may be any that keep to these rules, and one draw needn't show every extreme that they name: `tile_counts`: one device has all 128 slots live.
All inputs are finite; a program needn't handle non-finite values.
Results may differ from a plain program's by a relative error of at most 0.007.
Values may be sent and summed in bfloat16 or wider, within the bound.
No kernel may reach another device: no remote copies, remote signals or barrier semaphores. Data moves between devices by JAX's collectives and lax.ppermute only.
A program may use at most 64 MiB of HBM per device.

v0:
```python
import functools

import jax
import jax.numpy as jnp
from jax import lax
from jax.experimental import pallas as pl
from jax.experimental.pallas import tpu as pltpu
from jax.sharding import PartitionSpec as P

F32 = jnp.float32
BF16 = jnp.bfloat16
NT = (((1,), (1,)), ((), ()))
NN = (((1,), (0,)), ((), ()))
TB = 128
GX, GY, GZ = 4, 4, 8
ROWS = 256
FEAT = 256
CLASSES = 172
CPAD = 176
SLOTS = 128
FWD = 4
BWD = 2
UNROLL = 4
FWD_GROUPS = 52
BWD_GROUPS = 136
CHUNK = 1024
EARLY = 6
PLACE_OF_OFFSET = (7, 3, 4, 0, 1, 2, 5, 6)


def params(mib):
    return pltpu.CompilerParams(vmem_limit_bytes=mib * 1024 * 1024)


def vmem_spec():
    return pl.BlockSpec(memory_space=pltpu.VMEM)


def hbm_spec():
    return pl.BlockSpec(memory_space=pltpu.HBM)


def smem_spec():
    return pl.BlockSpec(memory_space=pltpu.SMEM)


def hold_kernel(tiles_hbm, after, tiles, sem):
    copy = pltpu.make_async_copy(tiles_hbm, tiles, sem)
    copy.start()
    copy.wait()


def hold_tiles(tiles, after):
    return pl.pallas_call(
        hold_kernel,
        name="hold_tiles",
        out_shape=jax.ShapeDtypeStruct(tiles.shape, tiles.dtype),
        in_specs=[hbm_spec(), vmem_spec()],
        out_specs=vmem_spec(),
        scratch_shapes=[pltpu.SemaphoreType.DMA],
        compiler_params=params(4),
        cost_estimate=pl.CostEstimate(flops=0, bytes_accessed=10**3, transcendentals=0),
    )(tiles, after)


def row_perm(move):
    pairs = []
    for index in range(GX * GY * 2):
        x, y, core = index // (2 * GY), (index // 2) % GY, index % 2
        x, y, core = move(x, y, core)
        pairs.append((index, ((x % GX) * GY + y % GY) * 2 + core))
    return pairs


def first_axis(step):
    return row_perm(lambda x, y, c: (x, y + step, c) if c == 0 else (x + step, y, c))


def second_axis(step):
    return row_perm(lambda x, y, c: (x + step, y, c) if c == 0 else (x, y + step, c))


def swap_core():
    return row_perm(lambda x, y, c: (x, y, 1 - c))


def gather_row(own, beside, relay):
    send = lambda v, perm: lax.ppermute(v, "row", perm)
    line = jnp.concatenate(
        [
            own,
            send(own, first_axis(-1)),
            send(own, first_axis(2)),
            send(own, first_axis(1)),
        ],
        0,
    )
    half = line.shape[0] // 2
    plus = send(line, second_axis(-1))
    minus = send(line, second_axis(1))
    if relay:
        late = [send(minus[:half], second_axis(1)), send(plus[half:], second_axis(-1))]
        line, plus, minus = lax.optimization_barrier((line, plus, minus))
    else:
        late = [send(line, second_axis(2))]
        line, plus = lax.optimization_barrier((line, plus))
    early = [line, plus, minus]
    early = early + [send(v, swap_core()) for v in early]
    late[-1], done = lax.optimization_barrier((late[-1], beside(early)))
    return early, late + [send(v, swap_core()) for v in late], done


def source_slots(col_ids):
    me = lax.axis_index("row")
    device = col_ids >> 1
    dx = ((device >> 3) - (me >> 3)) & (GX - 1)
    dy = ((device >> 1) - (me >> 1)) & (GY - 1)
    other = device & 1
    along_first = jnp.where(other == 0, dy, dx)
    along_second = jnp.where(other == 0, dx, dy)
    swapped = (other ^ me) & 1
    early = (swapped * 3 + jnp.where(along_second == 3, 2, along_second)) * 4
    line = jnp.where(along_second == 2, 24 + swapped * 4, early)
    return (line + along_first) * 2 + (col_ids & 1)


def along_col(value, step):
    return lax.ppermute(value, "col", [(i, (i + step) % GZ) for i in range(GZ)])


def gather_col(own):
    near = {d: along_col(own, -d if d < 4 else GZ - d) for d in (2, 6, 1, 7)}
    up = jnp.concatenate([near[1], near[2][:, :TB]], 1)
    down = jnp.concatenate([near[6][:, TB:], near[7]], 1)
    up, down = along_col(up, -2), along_col(down, 2)
    return [own] + [near[d] for d in (1, 2, 6, 7)], up, down


def gradient_slots(offset, half):
    early = jnp.where(offset > 5, offset - 3, offset) * 2 + half
    late = offset * 2 + half + 4
    is_late = (offset >= 3) & (offset <= 5)
    return jnp.where(is_late, late, early), is_late.astype(jnp.int32)


def reduce_col(up, down, late):
    up, down = along_col(up, 2), along_col(down, -2)
    one, two, six, seven = late()
    width = one.shape[1]
    half = jnp.zeros((one.shape[0], width // 2), F32)
    extra_up = jnp.concatenate([up[:, width:].astype(F32), half], 1)
    extra_down = jnp.concatenate([half, down[:, width:].astype(F32)], 1)
    return [
        along_col((two + extra_up).astype(BF16), 2),
        along_col((six + extra_down).astype(BF16), -2),
        along_col((one + up[:, :width].astype(F32)).astype(BF16), 1),
        along_col((seven + down[:, :width].astype(F32)).astype(BF16), -1),
    ]


def group_tiles(target, source, empty, count, n_targets, group, n_groups, early):
    slots = jnp.arange(SLOTS, dtype=jnp.int32)
    live = slots < count
    key = jnp.where(live, target, n_targets)
    targets = jnp.arange(n_targets, dtype=jnp.int32)
    members = jnp.sum((key[None, :] == targets[:, None]).astype(jnp.int32), 1)
    groups = (members + group - 1) >> (group.bit_length() - 1)
    n_early = jnp.sum(jnp.where(targets < early, groups, 0))
    n_early = (n_early + UNROLL - 1) & -UNROLL
    n_all = n_early + jnp.sum(jnp.where(targets >= early, groups, 0))
    before = (targets[None, :] < key[:, None]) & (
        (targets[None, :] >= early) == (key[:, None] >= early)
    )
    earlier = jnp.sum(jnp.where(before, groups[None, :], 0), 1)
    earlier = earlier + jnp.where(key >= early, n_early, 0)
    rank = jnp.sum(
        ((key[None, :] == key[:, None]) & (slots[None, :] < slots[:, None])).astype(jnp.int32), 1
    )
    place = jnp.where(live, earlier * group + rank, -1)
    places = jnp.arange(n_groups * group, dtype=jnp.int32)
    hit = place[None, :] == places[:, None]
    order = jnp.sum(jnp.where(hit, slots[None, :], 0), 1)
    picked = empty + jnp.sum(jnp.where(hit, source[None, :] - empty, 0), 1)
    first = place[None, :] == group * jnp.arange(n_groups, dtype=jnp.int32)[:, None]
    goal = jnp.sum(jnp.where(first, target[None, :], 0), 1)
    counts = jnp.where(jnp.arange(2) == 0, n_early, n_all)
    return order, picked, goal, counts


def run_groups(table, group, first, last, shift, product, total):
    order, picked, goal, _ = table

    def step(i, carry):
        made = []
        for u in range(UNROLL):
            start = (i * UNROLL + u) * group
            tiles = [order[start + k] for k in range(group)]
            sources = [picked[start + k] for k in range(group)]
            made.append(product(tiles, sources))
        for u in range(UNROLL):
            total[jnp.maximum(goal[i * UNROLL + u] - shift, 0)] += made[u]
        return carry

    lax.fori_loop(first // UNROLL, (last + UNROLL - 1) // UNROLL, step, 0)


def clear(ref):
    def step(i, carry):
        ref[i] = jnp.zeros(ref.shape[1:], ref.dtype)
        return carry

    lax.fori_loop(0, ref.shape[0], step, 0)


def copy_rows(piece, panel, start, rows):
    def step(i, carry):
        origin = pl.ds(pl.multiple_of(i * rows, rows), rows)
        target = pl.ds(pl.multiple_of(start + i * rows, rows), rows)
        panel[target, :] = piece[origin, :]
        return carry

    lax.fori_loop(0, piece.shape[0] // rows, step, 0)


def rows_product(tiles, source):
    def product(picked, origins):
        return lax.dot_general(
            jnp.concatenate([tiles[t] for t in picked], 1),
            jnp.concatenate([source[o] for o in origins], 0),
            NN,
            preferred_element_type=F32,
        )

    return product


def columns_product(tiles, source):
    def product(picked, origins):
        return lax.dot_general(
            jnp.concatenate([source[o] for o in origins], 1),
            jnp.concatenate([tiles[t] for t in picked], 1),
            NT,
            preferred_element_type=F32,
        )

    return product


def halves_of_rows(total, place):
    return jnp.concatenate([total[2 * place], total[2 * place + 1]], 0)


def halves_of_columns(total, place):
    return jnp.concatenate([total[2 * place], total[2 * place + 1]], 1)


def early_outputs(total, whole, out_up, out_down):
    far = whole(total, 1)
    width = far.shape[1]
    out_up[:, :width] = whole(total, 0).astype(BF16)
    out_up[:, width:] = far[:, : width // 2].astype(BF16)
    out_down[:, :width] = whole(total, 2).astype(BF16)
    out_down[:, width:] = far[:, width // 2 :].astype(BF16)


def aggregate_early_kernel(*refs):
    table, (tiles, *rest) = refs[:4], refs[4:]
    pieces, (source, out_up, out_down, total) = rest[:-4], rest[-4:]
    filled = 0
    for piece in pieces:

        def step(i, carry):
            source[filled + i] = piece[pl.ds(pl.multiple_of(i * TB, TB), TB), :]
            return carry

        lax.fori_loop(0, piece.shape[0] // TB, step, 0)
        filled += piece.shape[0] // TB
    source[filled] = jnp.zeros((TB, FEAT), BF16)
    clear(total)
    run_groups(table, FWD, 0, table[3][0], 0, rows_product(tiles, source), total)
    early_outputs(total, halves_of_rows, out_up, out_down)


def aggregate_late_kernel(*refs):
    table, (tiles, source, *rest) = refs[:4], refs[4:]
    outs, total = rest[:5], rest[5]
    clear(total)
    run_groups(table, FWD, table[3][0], table[3][1], EARLY, rows_product(tiles, source), total)
    for place, out in enumerate(outs):
        out[...] = halves_of_rows(total, place)


def sigmoid(value):
    return 0.5 * jnp.tanh(0.5 * value) + 0.5


def gates(pieces, weight_one_t, weight_two_t, source, agg, hidden_t, slope_t):
    filled = 0
    for piece in pieces:
        copy_rows(piece, agg, filled, ROWS)
        filled += piece.shape[0]

    def step(i, carry):
        span = pl.ds(pl.multiple_of(i * CHUNK, CHUNK), CHUNK)
        pre = lax.dot_general(weight_one_t[...], agg[span, :], NT, preferred_element_type=F32)
        gate = sigmoid(pre)
        hidden = (pre * gate).astype(BF16)
        hidden_t[:, span] = hidden
        slope_t[:, span] = (gate * (1.0 + pre * (1.0 - gate))).astype(BF16)
        projected = lax.dot_general(
            weight_two_t[...], hidden, NN, preferred_element_type=F32
        ).astype(BF16)
        for block in range(CHUNK // TB):
            source[i * (CHUNK // TB) + block] = projected[:, block * TB : (block + 1) * TB]
        return carry

    lax.fori_loop(0, filled // CHUNK, step, 0)


def panel_shapes(nodes):
    return (
        jax.ShapeDtypeStruct((nodes, FEAT), BF16),
        jax.ShapeDtypeStruct((FEAT, nodes), BF16),
        jax.ShapeDtypeStruct((FEAT, nodes), BF16),
    )


def gates_kernel(weight_one_t, weight_two_t, *rest):
    gates(rest[:-4], weight_one_t, weight_two_t, *rest[-4:])


def early_gates(weight_one_t, weight_two_t, pieces):
    nodes = sum(p.shape[0] for p in pieces)
    return pl.pallas_call(
        gates_kernel,
        name="early_gates",
        out_shape=(
            jax.ShapeDtypeStruct((nodes // TB, CPAD, TB), BF16),
            *panel_shapes(nodes),
        ),
        in_specs=[vmem_spec()] * (2 + len(pieces)),
        out_specs=[vmem_spec()] * 4,
        compiler_params=params(8),
        cost_estimate=pl.CostEstimate(flops=10**3, bytes_accessed=10**3, transcendentals=0),
    )(weight_one_t, weight_two_t, *pieces)


def logits_early_kernel(*refs):
    table, (tiles, weight_one_t, weight_two_t, begun, *rest) = refs[:4], refs[4:]
    pieces, rest = rest[:-7], rest[-7:]
    source, out_up, out_down, agg, hidden_t, slope_t, total = rest
    blocks = begun.shape[0]

    def step(i, carry):
        source[i] = begun[i]
        return carry

    lax.fori_loop(0, blocks, step, 0)
    later = source.at[pl.ds(blocks, 64 - blocks)]
    gates(pieces, weight_one_t, weight_two_t, later, agg, hidden_t, slope_t)
    source[64] = jnp.zeros((CPAD, TB), BF16)
    clear(total)
    run_groups(table, FWD, 0, table[3][0], 0, columns_product(tiles, source), total)
    early_outputs(total, halves_of_columns, out_up, out_down)


def logits_late_kernel(*refs):
    table, (tiles, source, *rest) = refs[:4], refs[4:]
    outs, total = rest[:5], rest[5]
    clear(total)
    run_groups(table, FWD, table[3][0], table[3][1], EARLY, columns_product(tiles, source), total)
    for place, out in enumerate(outs):
        out[...] = halves_of_columns(total, place)


def spread_and_reduce(early_kernel, late_kernel, name, table, operands, kept, block, out):
    cost = pl.CostEstimate(flops=10**9, bytes_accessed=10**7, transcendentals=0)
    wide = jax.ShapeDtypeStruct((out[0], out[1] * 3 // 2), BF16)
    source, up, down, *kept = pl.pallas_call(
        early_kernel,
        name=name + "_early",
        out_shape=(jax.ShapeDtypeStruct((65, *block), BF16), wide, wide, *kept),
        in_specs=[smem_spec()] * 4 + [vmem_spec()] * len(operands),
        out_specs=[vmem_spec()] * (3 + len(kept)),
        scratch_shapes=[pltpu.VMEM((EARLY, *block), F32)],
        compiler_params=params(10),
        cost_estimate=cost,
    )(*table, *operands)
    *late, own = pl.pallas_call(
        late_kernel,
        name=name + "_late",
        out_shape=(jax.ShapeDtypeStruct(out, F32),) * 5,
        in_specs=[smem_spec()] * 4 + [vmem_spec()] * 2,
        out_specs=[vmem_spec()] * 5,
        scratch_shapes=[pltpu.VMEM((16 - EARLY, *block), F32)],
        compiler_params=params(8),
        cost_estimate=cost,
    )(*table, operands[0], source)
    return [own] + reduce_col(up, down, lambda: late), kept


def add_up(parts):
    summed = parts[0][...].astype(F32)
    for part in parts[1:]:
        summed += part[...].astype(F32)
    return summed


def middle_kernel(*refs):
    parts, (one, two_t, agg, one_t, wide_t, wide, padded) = refs[:5], refs[5:]
    agg[...] = add_up(parts).astype(BF16)
    one_t[...] = jnp.transpose(one[...].astype(F32)).astype(BF16)
    padded[...] = jnp.zeros_like(padded)
    padded[0:CLASSES] = two_t[...].astype(F32)
    wide_t[...] = padded[...].astype(BF16)
    wide[...] = jnp.transpose(padded[...]).astype(BF16)


def middle(parts, weight_one, weight_two_t):
    return pl.pallas_call(
        middle_kernel,
        name="middle",
        out_shape=(
            jax.ShapeDtypeStruct((ROWS, FEAT), BF16),
            jax.ShapeDtypeStruct((FEAT, FEAT), BF16),
            jax.ShapeDtypeStruct((CPAD, FEAT), BF16),
            jax.ShapeDtypeStruct((FEAT, CPAD), BF16),
        ),
        in_specs=[vmem_spec()] * 7,
        out_specs=[vmem_spec()] * 4,
        scratch_shapes=[pltpu.VMEM((CPAD, FEAT), F32)],
        compiler_params=params(8),
    )(*parts, weight_one, weight_two_t)


def loss_kernel(scale, *refs):
    parts, (labels, place, logits_t, grad_t) = refs[:5], refs[5:]
    summed = add_up(parts)
    logits_t[...] = summed[:CLASSES]
    ids = lax.broadcasted_iota(jnp.int32, summed.shape, 0)
    valid = ids < CLASSES
    top = jnp.max(jnp.where(valid, summed, -jnp.inf), 0, keepdims=True)
    grown = jnp.where(valid, jnp.exp(summed - top), 0.0)
    soft = grown / jnp.sum(grown, 0, keepdims=True)
    own_labels = jnp.concatenate([labels[pl.ds(place[0] * 2 + k, 1), :] for k in range(2)], 1)
    onehot = (ids == own_labels).astype(F32)
    grad_t[...] = ((soft - onehot) * scale).astype(BF16)


def loss_grad(parts, labels, place, scale):
    return pl.pallas_call(
        functools.partial(loss_kernel, scale),
        name="loss_grad",
        out_shape=(
            jax.ShapeDtypeStruct((CLASSES, ROWS), F32),
            jax.ShapeDtypeStruct((CPAD, ROWS), BF16),
        ),
        in_specs=[vmem_spec()] * 6 + [smem_spec()],
        out_specs=[vmem_spec()] * 2,
        compiler_params=params(8),
    )(*parts, labels, place)


def backward_tiles(table, first, last, shift, tiles, grads, total):
    def product(picked, origins):
        return lax.dot_general(
            jnp.concatenate([grads[o] for o in origins], 1),
            jnp.concatenate([tiles[t] for t in picked], 0),
            NN,
            preferred_element_type=F32,
        )

    run_groups(table, BWD, first, last, shift, product, total)


def backward_early_kernel(*refs):
    table, (tiles, *pieces), (total, grads) = refs[:4], refs[4:-2], refs[-2:]
    for place, piece in enumerate(pieces):
        grads[2 * place] = piece[:, :TB]
        grads[2 * place + 1] = piece[:, TB:]
    grads[16] = jnp.zeros((CPAD, TB), BF16)
    clear(total)
    backward_tiles(table, 0, table[3][0], 0, tiles, grads, total)


def backward_early(table, tiles, pieces):
    return pl.pallas_call(
        backward_early_kernel,
        name="backward_early",
        out_shape=jax.ShapeDtypeStruct((64, CPAD, TB), F32),
        in_specs=[smem_spec()] * 4 + [vmem_spec()] * (1 + len(pieces)),
        out_specs=vmem_spec(),
        scratch_shapes=[pltpu.VMEM((17, CPAD, TB), BF16)],
        compiler_params=params(8),
        cost_estimate=pl.CostEstimate(flops=10**3, bytes_accessed=10**3, transcendentals=0),
    )(*table, tiles, *pieces)


def backward_late_kernel(*refs):
    table, (tiles, weight_two, begun, *rest) = refs[:4], refs[4:]
    panels, (up, down, *rest) = (rest[0:3], rest[3:6]), rest[6:]
    out, grads, total, sum_one, sum_two = rest
    for place, piece in enumerate((up, down)):
        for k in range(3):
            grads[10 + 3 * place + k] = piece[:, k * TB : (k + 1) * TB]
    grads[16] = jnp.zeros((CPAD, TB), BF16)

    def take(i, carry):
        total[i] = begun[i]
        return carry

    lax.fori_loop(0, 64, take, 0)
    backward_tiles(table, table[3][0], table[3][1], 64, tiles, grads, total)
    sum_one[...] = jnp.zeros_like(sum_one)
    sum_two[...] = jnp.zeros_like(sum_two)
    blocks = 8
    span = blocks * TB
    done = 0
    for agg, hidden, slope in panels:

        def finish(i, carry):
            held = [total[done + i * blocks + k] for k in range(blocks)]
            back = jnp.concatenate(held, 1).astype(BF16)
            part = pl.ds(pl.multiple_of(i * span, span), span)
            grad = lax.dot_general(weight_two[...], back, NN, preferred_element_type=F32)
            grad = (grad * slope[:, part].astype(F32)).astype(BF16)
            sum_one[...] += lax.dot_general(grad, agg[part, :], NN, preferred_element_type=F32)
            sum_two[...] += lax.dot_general(back, hidden[:, part], NT, preferred_element_type=F32)
            return carry

        lax.fori_loop(0, agg.shape[0] // span, finish, 0)
        done += agg.shape[0] // TB
    out[0:FEAT] = jnp.transpose(sum_one[...]).astype(BF16)
    out[FEAT : FEAT + CPAD] = sum_two[...].astype(BF16)
    out[FEAT + CPAD :] = jnp.zeros((512 - FEAT - CPAD, FEAT), BF16)


def backward_late(table, tiles, weight_two, begun, panels, up, down):
    return pl.pallas_call(
        backward_late_kernel,
        name="backward_late",
        out_shape=jax.ShapeDtypeStruct((512, FEAT), BF16),
        in_specs=[smem_spec()] * 4 + [vmem_spec()] * (5 + len(panels)),
        out_specs=vmem_spec(),
        scratch_shapes=[
            pltpu.VMEM((17, CPAD, TB), BF16),
            pltpu.VMEM((64, CPAD, TB), F32),
            pltpu.VMEM((FEAT, FEAT), F32),
            pltpu.VMEM((CPAD, FEAT), F32),
        ],
        compiler_params=params(12),
        cost_estimate=pl.CostEstimate(flops=5 * 10**9, bytes_accessed=2 * 10**7, transcendentals=0),
    )(*table, tiles, weight_two, begun, *panels, up, down)


def sum_everywhere(grads):
    shares = lax.all_to_all(grads.reshape(32, 16, FEAT), "row", 0, 0, tiled=True)
    share = jnp.sum(shares.astype(F32), 0).astype(BF16)
    shares = lax.all_to_all(
        jnp.broadcast_to(share, (GZ, 16, FEAT)), "col", 0, 0, tiled=True
    )
    share = jnp.sum(shares.astype(F32), 0).astype(BF16)
    full = lax.all_to_all(jnp.broadcast_to(share, (32, 16, FEAT)), "row", 0, 0, tiled=True)
    return full.reshape(512, FEAT)


def body(features, weight_one, weight_two, adj_tiles, tile_rows, tile_cols, tile_counts, labels):
    z = lax.axis_index("col")
    node_total = ROWS * lax.axis_size("row") * lax.axis_size("col")
    labels = labels.reshape(GZ * ROWS // TB, TB)
    place = jnp.full((1,), z, jnp.int32)
    second_t = weight_two.T

    def prepare(early):
        given = (tile_rows[0, 0], tile_cols[0, 0], tile_counts[0, 0], early[0])
        row_ids, col_ids, count, _ = lax.optimization_barrier(given)
        offset = ((row_ids >> 1) - z) & (GZ - 1)
        half = row_ids & 1
        rank = sum(jnp.where(offset == d, PLACE_OF_OFFSET[d], 0) for d in range(GZ))
        sources = source_slots(col_ids)
        forward = group_tiles(rank * 2 + half, sources, 64, count, 16, FWD, FWD_GROUPS, EARLY)
        slots, late = gradient_slots(offset, half)
        reverse = group_tiles(late * 64 + sources, slots, 16, count, 128, BWD, BWD_GROUPS, 64)
        ready = (forward, reverse, labels, place, adj_tiles[0, 0])
        *ready, tiles = lax.optimization_barrier(ready)
        return (*ready, hold_tiles(tiles, early[0]))

    early, late, done = gather_row(features, prepare, False)
    forward, reverse, labels, place, tiles = done
    parts, _ = spread_and_reduce(
        aggregate_early_kernel,
        aggregate_late_kernel,
        "aggregate",
        forward,
        (tiles, *early, *late),
        (),
        (TB, FEAT),
        (ROWS, FEAT),
    )
    agg, weight_one_t, weight_two_t, weight_two = middle(parts, weight_one, second_t)
    early, late, begun = gather_row(
        agg, functools.partial(early_gates, weight_one_t, weight_two_t), True
    )
    parts, panel = spread_and_reduce(
        logits_early_kernel,
        logits_late_kernel,
        "partial_logits",
        forward,
        (tiles, weight_one_t, weight_two_t, begun[0], *late),
        panel_shapes(sum(p.shape[0] for p in late)),
        (CPAD, TB),
        (CPAD, ROWS),
    )
    logits_t, grad_t = loss_grad(parts, labels, place, node_total ** (-0.5))
    near, up, down = gather_col(grad_t)
    total = backward_early(reverse, tiles, near)
    grads = backward_late(
        reverse, tiles, weight_two, total, (*begun[1:], *panel), up, down
    )
    grads = sum_everywhere(grads)
    grad_one = grads[:FEAT].astype(F32)
    grad_two = grads[FEAT : FEAT + CLASSES].astype(F32).T
    return logits_t.T, grad_one, grad_two


def solution(mesh):
    in_specs = (
        P(("row", "col"), None),
        P(),
        P(),
        P("row", "col", None, None, None),
        P("row", "col", None),
        P("row", "col", None),
        P("row", "col"),
        P("row"),
    )
    out_specs = (P(("row", "col"), None), P(), P())
    return jax.shard_map(body, mesh=mesh, in_specs=in_specs, out_specs=out_specs, check_vma=False)
```

profile of v0, /device:TPU:1, one launch (start us, length us, event | category | flops | bytes accessed | tf_op | source)
XLA Modules:
  0.0 203.2 jit_solution(12754105542439051621)
XLA Ops:
  0.6 3.4 %collective-permute-start = (bf16[256,256]{1,0:T(8,128)(2,1)}, bf16[256,256]{1,0:T(8,128)(2,1)S(1)}, u32[]{:S(2)}, u32[]{:S(2)}) collective-permute-start(bf16[256,256]{1,0:T(8,128)(2,1)} %param.8), channel_id=1, source_target_pairs={{0,48},{8,200},{16,0},{24,216},{32,16},{40,232},{48,32},{56,248},{... | collective-permute-start | bytes 393224 | tf_op jit(solution)/shard_map/ppermute | solution.py:88
  6.1 1.6 collective-permute-done
  7.7 2.0 collective-permute-done.1
  9.7 1.6 collective-permute-done.2
  11.3 2.5 %collective-permute-start.4 = (bf16[1024,256]{1,0:T(8,128)(2,1)S(1)}, bf16[1024,256]{1,0:T(8,128)(2,1)S(1)}, u32[]{:S(2)}, u32[]{:S(2)}) collective-permute-start(bf16[1024,256]{1,0:T(8,128)(2,1)S(1)} %constant_dynamic-update-slice_fusion.after.refs_5_), channel_id=1, source_target_pairs={{0,192},{8,56},{16,208},{24,8},{32,224},{40,24},{48,240},{56,40},{... | collective-permute-start | bytes 1572872 | tf_op jit(solution)/shard_map/ppermute | solution.py:88
  15.6 9.9 %collective-permute-done.4.refs_6_ = bf16[1024,256]{1,0:T(8,128)(2,1)S(1)} collective-permute-done((bf16[1024,256]{1,0:T(8,128)(2,1)S(1)}, bf16[1024,256]{1,0:T(8,128)(2,1)S(1)}, u32[]{:S(2)}, u32[]{:S(2)}) %collective-permute-start.4) | collective-permute-done | bytes 524320 | tf_op jit(solution)/shard_map/ppermute | solution.py:88
  27.2 3.0 %collective-permute-start.6 = (bf16[1024,256]{1,0:T(8,128)(2,1)S(1)}, bf16[1024,256]{1,0:T(8,128)(2,1)S(1)}, u32[]{:S(2)}, u32[]{:S(2)}) collective-permute-start(bf16[1024,256]{1,0:T(8,128)(2,1)S(1)} %constant_dynamic-update-slice_fusion.after.refs_5_), channel_id=1, source_target_pairs={{0,8},{8,0},{16,24},{24,16},{32,40},{40,32},{48,56},{56,48},{64,72... | collective-permute-start | bytes 1572872 | tf_op jit(solution)/shard_map/ppermute | solution.py:88
  35.2 2.2 %copy-done = bf16[1,1,128,128,128]{4,3,2,1,0:T(8,128)(2,1)S(1)} copy-done((bf16[1,1,128,128,128]{4,3,2,1,0:T(8,128)(2,1)S(1)}, bf16[1,1,128,128,128]{4,3,2,1,0:T(8,128)(2,1)}, u32[]{:S(2)}) %copy-start) | copy-done | bytes 4194328
  38.4 1.3 collective-permute-done.7.refs_9_
  41.2 2.1 %aggregate_early.1 = (bf16[65,128,256]{2,1,0:T(8,128)(2,1)S(1)}, bf16[256,384]{1,0:T(8,128)(2,1)S(1)}, bf16[256,384]{1,0:T(8,128)(2,1)S(1)}) custom-call(s32[208]{0:T(256)S(1)} %get-tuple-element.83.refs_0_, s32[208]{0:T(256)S(1)} %broadcast_add_fusion.1.refs_1_, s32[52]{0:T(128)S(1)} %select_reduce_fusion.6.refs_2_, s32[2]{0:T(128)S(1)} %get-tuple-element.86.refs_3_, ...), custom_call_target="tpu_custom_call" | custom-call | flops 1000000000 | bytes 10000000 | tf_op jit(solution)/shard_map/aggregate_early/pallas_call | solution.py:379
  43.3 3.4 %collective-permute-start.10 = (bf16[256,384]{1,0:T(8,128)(2,1)S(1)}, bf16[256,384]{1,0:T(8,128)(2,1)S(1)}, u32[]{:S(2)}, u32[]{:S(2)}) collective-permute-start(bf16[256,384]{1,0:T(8,128)(2,1)S(1)} %get-tuple-element.93), channel_id=1, source_target_pairs={{0,2},{1,3},{2,4},{3,5},{4,6},{5,7},{6,0},{7,1},{8,10},{9,11},{10,... | collective-permute-start | bytes 589832 | tf_op jit(solution)/shard_map/ppermute | solution.py:128
  46.6 2.5 %collective-permute-start.12 = (bf16[256,384]{1,0:T(8,128)(2,1)S(1)}, bf16[256,384]{1,0:T(8,128)(2,1)S(1)}, u32[]{:S(2)}, u32[]{:S(2)}) collective-permute-start(bf16[256,384]{1,0:T(8,128)(2,1)S(1)} %get-tuple-element.95), channel_id=1, source_target_pairs={{0,6},{1,7},{2,0},{3,1},{4,2},{5,3},{6,4},{7,5},{8,14},{9,15},{10,... | collective-permute-start | bytes 589832 | tf_op jit(solution)/shard_map/ppermute | solution.py:128
  49.1 2.1 %aggregate_late.1 = (f32[256,256]{1,0:T(8,128)S(1)}, f32[256,256]{1,0:T(8,128)S(1)}, f32[256,256]{1,0:T(8,128)S(1)}, f32[256,256]{1,0:T(8,128)S(1)}, f32[256,256]{1,0:T(8,128)S(1)}) custom-call(s32[208]{0:T(256)S(1)} %get-tuple-element.83.refs_0_, s32[208]{0:T(256)S(1)} %broadcast_add_fusion.1.refs_1_, s32[52]{0:T(128)S(1)} %select_reduce_fusion.6.refs_2_, ...), custom_call_target="tpu_custom_call" | custom-call | flops 1000000000 | bytes 10000000 | tf_op jit(solution)/shard_map/aggregate_late/pallas_call | solution.py:389
  51.2 4.6 %collective-permute-done.10 = bf16[256,384]{1,0:T(8,128)(2,1)S(1)} collective-permute-done((bf16[256,384]{1,0:T(8,128)(2,1)S(1)}, bf16[256,384]{1,0:T(8,128)(2,1)S(1)}, u32[]{:S(2)}, u32[]{:S(2)}) %collective-permute-start.10) | collective-permute-done | bytes 196640 | tf_op jit(solution)/shard_map/ppermute | solution.py:128
  55.9 3.3 %collective-permute-start.11 = (bf16[256,256]{1,0:T(8,128)(2,1)S(1)}, bf16[256,256]{1,0:T(8,128)(2,1)S(1)}, u32[]{:S(2)}, u32[]{:S(2)}) collective-permute-start(bf16[256,256]{1,0:T(8,128)(2,1)S(1)} %add_convert_fusion.3), channel_id=1, source_target_pairs={{0,2},{1,3},{2,4},{3,5},{4,6},{5,7},{6,0},{7,1},{8,10},{9,11},{10,... | collective-permute-start | bytes 393224 | tf_op jit(solution)/shard_map/ppermute | solution.py:128
  59.7 2.2 %collective-permute-start.13 = (bf16[256,256]{1,0:T(8,128)(2,1)S(1)}, bf16[256,256]{1,0:T(8,128)(2,1)S(1)}, u32[]{:S(2)}, u32[]{:S(2)}) collective-permute-start(bf16[256,256]{1,0:T(8,128)(2,1)S(1)} %add_convert_fusion.2), channel_id=1, source_target_pairs={{0,6},{1,7},{2,0},{3,1},{4,2},{5,3},{6,4},{7,5},{8,14},{9,15},{10,... | collective-permute-start | bytes 393224 | tf_op jit(solution)/shard_map/ppermute | solution.py:128
  62.9 2.2 %collective-permute-start.15 = (bf16[256,256]{1,0:T(8,128)(2,1)S(1)}, bf16[256,256]{1,0:T(8,128)(2,1)S(1)}, u32[]{:S(2)}, u32[]{:S(2)}) collective-permute-start(bf16[256,256]{1,0:T(8,128)(2,1)S(1)} %add_convert_fusion), channel_id=1, source_target_pairs={{0,7},{1,0},{2,1},{3,2},{4,3},{5,4},{6,5},{7,6},{8,15},{9,8},{10,9... | collective-permute-start | bytes 393224 | tf_op jit(solution)/shard_map/ppermute | solution.py:128
  65.0 5.2 %collective-permute-done.13.refs_2_ = bf16[256,256]{1,0:T(8,128)(2,1)S(1)} collective-permute-done((bf16[256,256]{1,0:T(8,128)(2,1)S(1)}, bf16[256,256]{1,0:T(8,128)(2,1)S(1)}, u32[]{:S(2)}, u32[]{:S(2)}) %collective-permute-start.13) | collective-permute-done | bytes 131104 | tf_op jit(solution)/shard_map/ppermute | solution.py:128
  70.3 1.1 collective-permute-done.15.refs_4_
  71.6 3.5 %collective-permute-start.16 = (bf16[256,256]{1,0:T(8,128)(2,1)S(1)}, bf16[256,256]{1,0:T(8,128)(2,1)S(1)}, u32[]{:S(2)}, u32[]{:S(2)}) collective-permute-start(bf16[256,256]{1,0:T(8,128)(2,1)S(1)} %get-tuple-element.100), channel_id=1, source_target_pairs={{0,48},{8,200},{16,0},{24,216},{32,16},{40,232},{48,32},{56,248},{... | collective-permute-start | bytes 393224 | tf_op jit(solution)/shard_map/ppermute | solution.py:88
  75.9 2.5 %collective-permute-done.16 = bf16[256,256]{1,0:T(8,128)(2,1)S(1)} collective-permute-done((bf16[256,256]{1,0:T(8,128)(2,1)S(1)}, bf16[256,256]{1,0:T(8,128)(2,1)S(1)}, u32[]{:S(2)}, u32[]{:S(2)}) %collective-permute-start.16) | collective-permute-done | bytes 131104 | tf_op jit(solution)/shard_map/ppermute | solution.py:88
  78.5 2.1 %collective-permute-done.17 = bf16[256,256]{1,0:T(8,128)(2,1)S(1)} collective-permute-done((bf16[256,256]{1,0:T(8,128)(2,1)S(1)}, bf16[256,256]{1,0:T(8,128)(2,1)S(1)}, u32[]{:S(2)}, u32[]{:S(2)}) %collective-permute-start.17) | collective-permute-done | bytes 131104 | tf_op jit(solution)/shard_map/ppermute | solution.py:88
  83.2 6.9 %collective-permute-done.19.rest_1_ = bf16[1024,256]{1,0:T(8,128)(2,1)S(1)} collective-permute-done((bf16[1024,256]{1,0:T(8,128)(2,1)S(1)}, bf16[1024,256]{1,0:T(8,128)(2,1)S(1)}, u32[]{:S(2)}, u32[]{:S(2)}) %collective-permute-start.19) | collective-permute-done | bytes 524320 | tf_op jit(solution)/shard_map/ppermute | solution.py:88
  90.1 2.1 %collective-permute-done.21.rest_2_ = bf16[1024,256]{1,0:T(8,128)(2,1)S(1)} collective-permute-done((bf16[1024,256]{1,0:T(8,128)(2,1)S(1)}, bf16[1024,256]{1,0:T(8,128)(2,1)S(1)}, u32[]{:S(2)}, u32[]{:S(2)}) %collective-permute-start.21) | collective-permute-done | bytes 524320 | tf_op jit(solution)/shard_map/ppermute | solution.py:88
  92.2 4.2 %collective-permute-start.22 = (bf16[1024,256]{1,0:T(8,128)(2,1)S(1)}, bf16[1024,256]{1,0:T(8,128)(2,1)S(1)}, u32[]{:S(2)}, u32[]{:S(2)}) collective-permute-start(bf16[1024,256]{1,0:T(8,128)(2,1)S(1)} %constant_dynamic-update-slice_fusion.4.rest_0_), channel_id=1, source_target_pairs={{0,8},{8,0},{16,24},{24,16},{32,40},{40,32},{48,56},{56,48},{64,72... | collective-permute-start | bytes 1572872 | tf_op jit(solution)/shard_map/ppermute | solution.py:88
  97.1 2.7 %collective-permute-start.20 = (bf16[512,256]{1,0:T(8,128)(2,1)S(1)}, bf16[512,256]{1,0:T(8,128)(2,1)S(1)}, u32[]{:S(2)}, u32[]{:S(2)}) collective-permute-start(bf16[512,256]{1,0:T(8,128)(2,1)S(1)} %slice.61), channel_id=1, source_target_pairs={{0,192},{8,56},{16,208},{24,8},{32,224},{40,24},{48,240},{56,40},{... | collective-permute-start | bytes 786440 | tf_op jit(solution)/shard_map/ppermute | solution.py:88
  99.8 4.0 %collective-permute-done.25.refs_8_ = bf16[512,256]{1,0:T(8,128)(2,1)S(1)} collective-permute-done((bf16[512,256]{1,0:T(8,128)(2,1)S(1)}, bf16[512,256]{1,0:T(8,128)(2,1)S(1)}, u32[]{:S(2)}, u32[]{:S(2)}) %collective-permute-start.25) | collective-permute-done | bytes 262176 | tf_op jit(solution)/shard_map/ppermute | solution.py:88
  104.6 4.9 %early_gates.1 = (bf16[48,176,128]{2,1,0:T(8,128)(2,1)S(1)}, bf16[6144,256]{1,0:T(8,128)(2,1)S(1)}, bf16[256,6144]{1,0:T(8,128)(2,1)S(1)}, bf16[256,6144]{1,0:T(8,128)(2,1)S(1)}) custom-call(bf16[256,256]{1,0:T(8,128)(2,1)S(1)} %get-tuple-element.98.weight_one_t.refs_5_, bf16[176,256]{1,0:T(8,128)(2,1)S(1)} %get-tuple-element.99.weight_two_t.refs_6_, ...), custom_call_target="tpu_custom_call" | custom-call | flops 1000 | bytes 1000 | tf_op jit(solution)/shard_map/early_gates/pallas_call | solution.py:334
  109.7 1.5 collective-permute-done.27.refs_11_
  111.2 3.6 %partial_logits_early.1 = (bf16[65,176,128]{2,1,0:T(8,128)(2,1)S(1)}, bf16[176,384]{1,0:T(8,128)(2,1)S(1)}, bf16[176,384]{1,0:T(8,128)(2,1)S(1)}, bf16[2048,256]...) custom-call(s32[208]{0:T(256)S(1)} %get-tuple-element.83.refs_0_, ...), custom_call_target="tpu_custom_call" | custom-call | flops 1000000000 | bytes 10000000 | tf_op jit(solution)/shard_map/partial_logits_early/pallas_call | solution.py:379
  114.8 1.4 collective-permute-start.28
  116.2 2.2 %collective-permute-start.30 = (bf16[176,384]{1,0:T(8,128)(2,1)S(1)}, bf16[176,384]{1,0:T(8,128)(2,1)S(1)}, u32[]{:S(2)}, u32[]{:S(2)}) collective-permute-start(bf16[176,384]{1,0:T(8,128)(2,1)S(1)} %get-tuple-element.115), channel_id=1, source_target_pairs={{0,6},{1,7},{2,0},{3,1},{4,2},{5,3},{6,4},{7,5},{8,14},{9,15},{10,... | collective-permute-start | bytes 405512 | tf_op jit(solution)/shard_map/ppermute | solution.py:128
  118.5 2.1 %partial_logits_late.1 = (f32[176,256]{1,0:T(8,128)S(1)}, f32[176,256]{1,0:T(8,128)S(1)}, f32[176,256]{1,0:T(8,128)S(1)}, f32[176,256]{1,0:T(8,128)S(1)}, f32[176,256]{1,0:T(8,128)S(1)}) custom-call(s32[208]{0:T(256)S(1)} %get-tuple-element.83.refs_0_, s32[208]{0:T(256)S(1)} %broadcast_add_fusion.1.refs_1_, s32[52]{0:T(128)S(1)} %select_reduce_fusion.6.refs_2_, ...), custom_call_target="tpu_custom_call" | custom-call | flops 1000000000 | bytes 10000000 | tf_op jit(solution)/shard_map/partial_logits_late/pallas_call | solution.py:389
  120.6 4.3 %collective-permute-done.28 = bf16[176,384]{1,0:T(8,128)(2,1)S(1)} collective-permute-done((bf16[176,384]{1,0:T(8,128)(2,1)S(1)}, bf16[176,384]{1,0:T(8,128)(2,1)S(1)}, u32[]{:S(2)}, u32[]{:S(2)}) %collective-permute-start.28) | collective-permute-done | bytes 135200 | tf_op jit(solution)/shard_map/ppermute | solution.py:128
  125.8 3.2 %collective-permute-start.31 = (bf16[176,256]{1,0:T(8,128)(2,1)S(1)}, bf16[176,256]{1,0:T(8,128)(2,1)S(1)}, u32[]{:S(2)}, u32[]{:S(2)}) collective-permute-start(bf16[176,256]{1,0:T(8,128)(2,1)S(1)} %add_convert_fusion.6), channel_id=1, source_target_pairs={{0,6},{1,7},{2,0},{3,1},{4,2},{5,3},{6,4},{7,5},{8,14},{9,15},{10,... | collective-permute-start | bytes 270344 | tf_op jit(solution)/shard_map/ppermute | solution.py:128
  129.1 2.7 %collective-permute-start.33 = (bf16[176,256]{1,0:T(8,128)(2,1)S(1)}, bf16[176,256]{1,0:T(8,128)(2,1)S(1)}, u32[]{:S(2)}, u32[]{:S(2)}) collective-permute-start(bf16[176,256]{1,0:T(8,128)(2,1)S(1)} %add_convert_fusion.4), channel_id=1, source_target_pairs={{0,7},{1,0},{2,1},{3,2},{4,3},{5,4},{6,5},{7,6},{8,15},{9,8},{10,9... | collective-permute-start | bytes 270344 | tf_op jit(solution)/shard_map/ppermute | solution.py:128
  131.8 1.5 collective-permute-done.29.refs_1_
  135.4 2.2 %collective-permute-start.35 = (bf16[176,256]{1,0:T(8,128)(2,1)S(1)}, bf16[176,256]{1,0:T(8,128)(2,1)S(1)}, u32[]{:S(2)}, u32[]{:S(2)}) collective-permute-start(bf16[176,256]{1,0:T(8,128)(2,1)S(1)} %get-tuple-element.126.refs_5_), channel_id=1, source_target_pairs={{0,6},{1,7},{2,0},{3,1},{4,2},{5,3},{6,4},{7,5},{8,14},{9,15},{10,... | collective-permute-start | bytes 270344 | tf_op jit(solution)/shard_map/ppermute | solution.py:128
  137.5 2.0 collective-permute-start.36
  139.5 1.2 collective-permute-done.35.refs_7_
  140.7 2.2 %collective-permute-done.34.refs_6_ = bf16[176,256]{1,0:T(8,128)(2,1)S(1)} collective-permute-done((bf16[176,256]{1,0:T(8,128)(2,1)S(1)}, bf16[176,256]{1,0:T(8,128)(2,1)S(1)}, u32[]{:S(2)}, u32[]{:S(2)}) %collective-permute-start.34) | collective-permute-done | bytes 90144 | tf_op jit(solution)/shard_map/ppermute | solution.py:128
  143.8 1.4 collective-permute-done.37.refs_9_
  145.7 3.5 %backward_early.1.refs_6_ = f32[64,176,128]{2,1,0:T(8,128)S(1)} custom-call(s32[272]{0:T(512)S(1)} %get-tuple-element.121.refs_0_, s32[272]{0:T(512)S(1)} %broadcast_add_fusion.refs_1_, s32[136]{0:T(256)S(1)} %select_reduce_fusion.4.refs_2_, s32[2]{0:T(128)S(1)} %get-tuple-element.124.refs_3_, bf16[128,128,128]{2,1,0:T(8,128)(2,1)S(1)} %hold_tiles.1.refs_4_, ...), custom_call_target="tpu_custom_call" | custom-call | flops 1000 | bytes 1000 | tf_op jit(solution)/shard_map/backward_early/pallas_call | solution.py:487
  149.2 2.4 %collective-permute-done.39.refs_14_ = bf16[176,384]{1,0:T(8,128)(2,1)S(1)} collective-permute-done((bf16[176,384]{1,0:T(8,128)(2,1)S(1)}, bf16[176,384]{1,0:T(8,128)(2,1)S(1)}, u32[]{:S(2)}, u32[]{:S(2)}) %collective-permute-start.39) | collective-permute-done | bytes 135200 | tf_op jit(solution)/shard_map/ppermute | solution.py:128
  151.6 8.1 %backward_late.1 = bf16[512,256]{1,0:T(8,128)(2,1)S(1)} custom-call(s32[272]{0:T(512)S(1)} %get-tuple-element.121.refs_0_, s32[272]{0:T(512)S(1)} %broadcast_add_fusion.refs_1_, s32[136]{0:T(256)S(1)} %select_reduce_fusion.4.refs_2_, s32[2]{0:T(128)S(1)} %get-tuple-element.124.refs_3_, bf16[128,128,128]{2,1,0:T(8,128)(2,1)S(1)} %hold_tiles.1.refs_4_, ...), custom_call_target="tpu_custom_call" | custom-call | flops 5000000000 | bytes 20000000 | tf_op jit(solution)/shard_map/backward_late/pallas_call | solution.py:539
  159.7 17.8 %all_to_all.15 = bf16[32,16,256]{2,1,0:T(8,128)(2,1)S(1)} all-to-all(bf16[32,16,256]{2,1,0:T(8,128)(2,1)S(1)} %bitcast.18), channel_id=1, replica_groups=mesh['row'=32,'col'=8] {'row'}, dimensions={0} | all-to-all | bytes 524288 | tf_op jit(solution)/shard_map/all_to_all | solution.py:557
  177.5 10.3 %all_to_all.16 = bf16[8,16,256]{2,1,0:T(8,128)(2,1)S(1)} all-to-all(bf16[8,16,256]{2,1,0:T(8,128)(2,1)S(1)} %broadcast_in_dim.224), channel_id=1, replica_groups=mesh['row'=32,'col'=8] {'col'}, dimensions={0} | all-to-all | bytes 131072 | tf_op jit(solution)/shard_map/all_to_all | solution.py:559
  187.8 13.9 %all_to_all.17 = bf16[32,16,256]{2,1,0:T(8,128)(2,1)S(1)} all-to-all(bf16[32,16,256]{2,1,0:T(8,128)(2,1)S(1)} %broadcast_in_dim.225), channel_id=1, replica_groups=mesh['row'=32,'col'=8] {'row'}, dimensions={0} | all-to-all | bytes 524288 | tf_op jit(solution)/shard_map/all_to_all | solution.py:563
  (108 shorter events, 22.4 us)
Async XLA Ops:
  0.6 7.1 %collective-permute-start = (bf16[256,256]{1,0:T(8,128)(2,1)}, bf16[256,256]{1,0:T(8,128)(2,1)S(1)}, u32[]{:S(2)}, u32[]{:S(2)}) collective-permute-start(bf16[256,256]{1,0:T(8,128)(2,1)} %param.8), channel_id=1, source_target_pairs={{0,48},{8,200},{16,0},{24,216},{32,16},{40,232},{48,32},{56,248},{... | collective-permute-start | bytes 393224 | tf_op jit(solution)/shard_map/ppermute | solution.py:88
  4.0 5.6 %collective-permute-start.1 = (bf16[256,256]{1,0:T(8,128)(2,1)}, bf16[256,256]{1,0:T(8,128)(2,1)S(1)}, u32[]{:S(2)}, u32[]{:S(2)}) collective-permute-start(bf16[256,256]{1,0:T(8,128)(2,1)} %param.8), channel_id=1, source_target_pairs={{0,32},{8,136},{16,48},{24,152},{32,0},{40,168},{48,16},{56,184},{... | collective-permute-start | bytes 393224 | tf_op jit(solution)/shard_map/ppermute | solution.py:88
  4.5 6.7 %collective-permute-start.2 = (bf16[256,256]{1,0:T(8,128)(2,1)}, bf16[256,256]{1,0:T(8,128)(2,1)S(1)}, u32[]{:S(2)}, u32[]{:S(2)}) collective-permute-start(bf16[256,256]{1,0:T(8,128)(2,1)} %param.8), channel_id=1, source_target_pairs={{0,16},{8,72},{16,32},{24,88},{32,48},{40,104},{48,0},{56,120},{64... | collective-permute-start | bytes 393224 | tf_op jit(solution)/shard_map/ppermute | solution.py:88
  11.3 14.3 %collective-permute-start.4 = (bf16[1024,256]{1,0:T(8,128)(2,1)S(1)}, bf16[1024,256]{1,0:T(8,128)(2,1)S(1)}, u32[]{:S(2)}, u32[]{:S(2)}) collective-permute-start(bf16[1024,256]{1,0:T(8,128)(2,1)S(1)} %constant_dynamic-update-slice_fusion.after.refs_5_), channel_id=1, source_target_pairs={{0,192},{8,56},{16,208},{24,8},{32,224},{40,24},{48,240},{56,40},{... | collective-permute-start | bytes 1572872 | tf_op jit(solution)/shard_map/ppermute | solution.py:88
  14.5 23.2 %collective-permute-start.3 = (bf16[1024,256]{1,0:T(8,128)(2,1)S(1)}, bf16[1024,256]{1,0:T(8,128)(2,1)S(1)}, u32[]{:S(2)}, u32[]{:S(2)}) collective-permute-start(bf16[1024,256]{1,0:T(8,128)(2,1)S(1)} %constant_dynamic-update-slice_fusion.after.refs_5_), channel_id=1, source_target_pairs={{0,128},{8,40},{16,144},{24,56},{32,160},{40,8},{48,176},{56,24},{... | collective-permute-start | bytes 1572872 | tf_op jit(solution)/shard_map/ppermute | solution.py:88
  14.9 22.9 %collective-permute-start.5 = (bf16[1024,256]{1,0:T(8,128)(2,1)S(1)}, bf16[1024,256]{1,0:T(8,128)(2,1)S(1)}, u32[]{:S(2)}, u32[]{:S(2)}) collective-permute-start(bf16[1024,256]{1,0:T(8,128)(2,1)S(1)} %constant_dynamic-update-slice_fusion.after.refs_5_), channel_id=1, source_target_pairs={{0,64},{8,24},{16,80},{24,40},{32,96},{40,56},{48,112},{56,8},{64,... | collective-permute-start | bytes 1572872 | tf_op jit(solution)/shard_map/ppermute | solution.py:88
  27.2 11.2 %collective-permute-start.6 = (bf16[1024,256]{1,0:T(8,128)(2,1)S(1)}, bf16[1024,256]{1,0:T(8,128)(2,1)S(1)}, u32[]{:S(2)}, u32[]{:S(2)}) collective-permute-start(bf16[1024,256]{1,0:T(8,128)(2,1)S(1)} %constant_dynamic-update-slice_fusion.after.refs_5_), channel_id=1, source_target_pairs={{0,8},{8,0},{16,24},{24,16},{32,40},{40,32},{48,56},{56,48},{64,72... | collective-permute-start | bytes 1572872 | tf_op jit(solution)/shard_map/ppermute | solution.py:88
  35.2 2.2 %copy-start = (bf16[1,1,128,128,128]{4,3,2,1,0:T(8,128)(2,1)S(1)}, bf16[1,1,128,128,128]{4,3,2,1,0:T(8,128)(2,1)}, u32[]{:S(2)}) copy-start(bf16[1,1,128,128,128]{4,3,2,1,0:T(8,128)(2,1)} %param.11) | copy-start | bytes 12582916
  37.7 2.0 collective-permute-start.7
  37.8 2.6 %collective-permute-start.8 = (bf16[1024,256]{1,0:T(8,128)(2,1)S(1)}, bf16[1024,256]{1,0:T(8,128)(2,1)S(1)}, u32[]{:S(2)}, u32[]{:S(2)}) collective-permute-start(bf16[1024,256]{1,0:T(8,128)(2,1)S(1)} %collective-permute-done.5.refs_7_), channel_id=1, source_target_pairs={{0,8},{8,0},{16,24},{24,16},{32,40},{40,32},{48,56},{56,48},{64,72... | collective-permute-start | bytes 1572872 | tf_op jit(solution)/shard_map/ppermute | solution.py:88
  38.3 2.9 %collective-permute-start.9 = (bf16[1024,256]{1,0:T(8,128)(2,1)S(1)}, bf16[1024,256]{1,0:T(8,128)(2,1)S(1)}, u32[]{:S(2)}, u32[]{:S(2)}) collective-permute-start(bf16[1024,256]{1,0:T(8,128)(2,1)S(1)} %collective-permute-done.3.refs_11_), channel_id=1, source_target_pairs={{0,8},{8,0},{16,24},{24,16},{32,40},{40,32},{48,56},{56,48},{64,72... | collective-permute-start | bytes 1572872 | tf_op jit(solution)/shard_map/ppermute | solution.py:88
  43.3 12.6 %collective-permute-start.10 = (bf16[256,384]{1,0:T(8,128)(2,1)S(1)}, bf16[256,384]{1,0:T(8,128)(2,1)S(1)}, u32[]{:S(2)}, u32[]{:S(2)}) collective-permute-start(bf16[256,384]{1,0:T(8,128)(2,1)S(1)} %get-tuple-element.93), channel_id=1, source_target_pairs={{0,2},{1,3},{2,4},{3,5},{4,6},{5,7},{6,0},{7,1},{8,10},{9,11},{10,... | collective-permute-start | bytes 589832 | tf_op jit(solution)/shard_map/ppermute | solution.py:128
  46.6 13.1 %collective-permute-start.12 = (bf16[256,384]{1,0:T(8,128)(2,1)S(1)}, bf16[256,384]{1,0:T(8,128)(2,1)S(1)}, u32[]{:S(2)}, u32[]{:S(2)}) collective-permute-start(bf16[256,384]{1,0:T(8,128)(2,1)S(1)} %get-tuple-element.95), channel_id=1, source_target_pairs={{0,6},{1,7},{2,0},{3,1},{4,2},{5,3},{6,4},{7,5},{8,14},{9,15},{10,... | collective-permute-start | bytes 589832 | tf_op jit(solution)/shard_map/ppermute | solution.py:128
  49.1 22.3 %copy-start.1 = (bf16[256,256]{1,0:T(8,128)(2,1)S(1)}, bf16[256,256]{1,0:T(8,128)(2,1)}, u32[]{:S(2)}) copy-start(bf16[256,256]{1,0:T(8,128)(2,1)} %refs_5_.1) | copy-start | bytes 393220
  49.1 22.3 %copy-start.2 = (bf16[256,172]{0,1:T(8,128)(2,1)S(1)}, bf16[256,172]{0,1:T(8,128)(2,1)}, u32[]{:S(2)}) copy-start(bf16[256,172]{0,1:T(8,128)(2,1)} %param.10) | copy-start | bytes 264196
  55.9 9.2 %collective-permute-start.11 = (bf16[256,256]{1,0:T(8,128)(2,1)S(1)}, bf16[256,256]{1,0:T(8,128)(2,1)S(1)}, u32[]{:S(2)}, u32[]{:S(2)}) collective-permute-start(bf16[256,256]{1,0:T(8,128)(2,1)S(1)} %add_convert_fusion.3), channel_id=1, source_target_pairs={{0,2},{1,3},{2,4},{3,5},{4,6},{5,7},{6,0},{7,1},{8,10},{9,11},{10,... | collective-permute-start | bytes 393224 | tf_op jit(solution)/shard_map/ppermute | solution.py:128
  59.7 10.5 %collective-permute-start.13 = (bf16[256,256]{1,0:T(8,128)(2,1)S(1)}, bf16[256,256]{1,0:T(8,128)(2,1)S(1)}, u32[]{:S(2)}, u32[]{:S(2)}) collective-permute-start(bf16[256,256]{1,0:T(8,128)(2,1)S(1)} %add_convert_fusion.2), channel_id=1, source_target_pairs={{0,6},{1,7},{2,0},{3,1},{4,2},{5,3},{6,4},{7,5},{8,14},{9,15},{10,... | collective-permute-start | bytes 393224 | tf_op jit(solution)/shard_map/ppermute | solution.py:128
  62.0 8.3 %collective-permute-start.14 = (bf16[256,256]{1,0:T(8,128)(2,1)S(1)}, bf16[256,256]{1,0:T(8,128)(2,1)S(1)}, u32[]{:S(2)}, u32[]{:S(2)}) collective-permute-start(bf16[256,256]{1,0:T(8,128)(2,1)S(1)} %add_convert_fusion.1), channel_id=1, source_target_pairs={{0,1},{1,2},{2,3},{3,4},{4,5},{5,6},{6,7},{7,0},{8,9},{9,10},{10,1... | collective-permute-start | bytes 393224 | tf_op jit(solution)/shard_map/ppermute | solution.py:128
  62.9 8.5 %collective-permute-start.15 = (bf16[256,256]{1,0:T(8,128)(2,1)S(1)}, bf16[256,256]{1,0:T(8,128)(2,1)S(1)}, u32[]{:S(2)}, u32[]{:S(2)}) collective-permute-start(bf16[256,256]{1,0:T(8,128)(2,1)S(1)} %add_convert_fusion), channel_id=1, source_target_pairs={{0,7},{1,0},{2,1},{3,2},{4,3},{5,4},{6,5},{7,6},{8,15},{9,8},{10,9... | collective-permute-start | bytes 393224 | tf_op jit(solution)/shard_map/ppermute | solution.py:128
  71.6 6.9 %collective-permute-start.16 = (bf16[256,256]{1,0:T(8,128)(2,1)S(1)}, bf16[256,256]{1,0:T(8,128)(2,1)S(1)}, u32[]{:S(2)}, u32[]{:S(2)}) collective-permute-start(bf16[256,256]{1,0:T(8,128)(2,1)S(1)} %get-tuple-element.100), channel_id=1, source_target_pairs={{0,48},{8,200},{16,0},{24,216},{32,16},{40,232},{48,32},{56,248},{... | collective-permute-start | bytes 393224 | tf_op jit(solution)/shard_map/ppermute | solution.py:88
  75.1 5.4 %collective-permute-start.17 = (bf16[256,256]{1,0:T(8,128)(2,1)S(1)}, bf16[256,256]{1,0:T(8,128)(2,1)S(1)}, u32[]{:S(2)}, u32[]{:S(2)}) collective-permute-start(bf16[256,256]{1,0:T(8,128)(2,1)S(1)} %get-tuple-element.100), channel_id=1, source_target_pairs={{0,32},{8,136},{16,48},{24,152},{32,0},{40,168},{48,16},{56,184},{... | collective-permute-start | bytes 393224 | tf_op jit(solution)/shard_map/ppermute | solution.py:88
  75.1 6.5 %collective-permute-start.18 = (bf16[256,256]{1,0:T(8,128)(2,1)S(1)}, bf16[256,256]{1,0:T(8,128)(2,1)S(1)}, u32[]{:S(2)}, u32[]{:S(2)}) collective-permute-start(bf16[256,256]{1,0:T(8,128)(2,1)S(1)} %get-tuple-element.100), channel_id=1, source_target_pairs={{0,16},{8,72},{16,32},{24,88},{32,48},{40,104},{48,0},{56,120},{64... | collective-permute-start | bytes 393224 | tf_op jit(solution)/shard_map/ppermute | solution.py:88
  81.7 8.4 %collective-permute-start.19 = (bf16[1024,256]{1,0:T(8,128)(2,1)S(1)}, bf16[1024,256]{1,0:T(8,128)(2,1)S(1)}, u32[]{:S(2)}, u32[]{:S(2)}) collective-permute-start(bf16[1024,256]{1,0:T(8,128)(2,1)S(1)} %constant_dynamic-update-slice_fusion.4.rest_0_), channel_id=1, source_target_pairs={{0,192},{8,56},{16,208},{24,8},{32,224},{40,24},{48,240},{56,40},{... | collective-permute-start | bytes 1572872 | tf_op jit(solution)/shard_map/ppermute | solution.py:88
  82.7 9.5 %collective-permute-start.21 = (bf16[1024,256]{1,0:T(8,128)(2,1)S(1)}, bf16[1024,256]{1,0:T(8,128)(2,1)S(1)}, u32[]{:S(2)}, u32[]{:S(2)}) collective-permute-start(bf16[1024,256]{1,0:T(8,128)(2,1)S(1)} %constant_dynamic-update-slice_fusion.4.rest_0_), channel_id=1, source_target_pairs={{0,64},{8,24},{16,80},{24,40},{32,96},{40,56},{48,112},{56,8},{64,... | collective-permute-start | bytes 1572872 | tf_op jit(solution)/shard_map/ppermute | solution.py:88
  92.2 12.4 %collective-permute-start.22 = (bf16[1024,256]{1,0:T(8,128)(2,1)S(1)}, bf16[1024,256]{1,0:T(8,128)(2,1)S(1)}, u32[]{:S(2)}, u32[]{:S(2)}) collective-permute-start(bf16[1024,256]{1,0:T(8,128)(2,1)S(1)} %constant_dynamic-update-slice_fusion.4.rest_0_), channel_id=1, source_target_pairs={{0,8},{8,0},{16,24},{24,16},{32,40},{40,32},{48,56},{56,48},{64,72... | collective-permute-start | bytes 1572872 | tf_op jit(solution)/shard_map/ppermute | solution.py:88
  96.4 8.2 %collective-permute-start.23 = (bf16[1024,256]{1,0:T(8,128)(2,1)S(1)}, bf16[1024,256]{1,0:T(8,128)(2,1)S(1)}, u32[]{:S(2)}, u32[]{:S(2)}) collective-permute-start(bf16[1024,256]{1,0:T(8,128)(2,1)S(1)} %collective-permute-done.19.rest_1_), channel_id=1, source_target_pairs={{0,8},{8,0},{16,24},{24,16},{32,40},{40,32},{48,56},{56,48},{64,72... | collective-permute-start | bytes 1572872 | tf_op jit(solution)/shard_map/ppermute | solution.py:88
  96.4 8.2 %collective-permute-start.24 = (bf16[1024,256]{1,0:T(8,128)(2,1)S(1)}, bf16[1024,256]{1,0:T(8,128)(2,1)S(1)}, u32[]{:S(2)}, u32[]{:S(2)}) collective-permute-start(bf16[1024,256]{1,0:T(8,128)(2,1)S(1)} %collective-permute-done.21.rest_2_), channel_id=1, source_target_pairs={{0,8},{8,0},{16,24},{24,16},{32,40},{40,32},{48,56},{56,48},{64,72... | collective-permute-start | bytes 1572872 | tf_op jit(solution)/shard_map/ppermute | solution.py:88
  96.9 6.8 %collective-permute-start.25 = (bf16[512,256]{1,0:T(8,128)(2,1)S(1)}, bf16[512,256]{1,0:T(8,128)(2,1)S(1)}, u32[]{:S(2)}, u32[]{:S(2)}) collective-permute-start(bf16[512,256]{1,0:T(8,128)(2,1)S(1)} %slice.62), channel_id=1, source_target_pairs={{0,64},{8,24},{16,80},{24,40},{32,96},{40,56},{48,112},{56,8},{64,... | collective-permute-start | bytes 786440 | tf_op jit(solution)/shard_map/ppermute | solution.py:88
  97.1 12.5 %collective-permute-start.20 = (bf16[512,256]{1,0:T(8,128)(2,1)S(1)}, bf16[512,256]{1,0:T(8,128)(2,1)S(1)}, u32[]{:S(2)}, u32[]{:S(2)}) collective-permute-start(bf16[512,256]{1,0:T(8,128)(2,1)S(1)} %slice.61), channel_id=1, source_target_pairs={{0,192},{8,56},{16,208},{24,8},{32,224},{40,24},{48,240},{56,40},{... | collective-permute-start | bytes 786440 | tf_op jit(solution)/shard_map/ppermute | solution.py:88
  103.7 5.9 %collective-permute-start.26 = (bf16[512,256]{1,0:T(8,128)(2,1)S(1)}, bf16[512,256]{1,0:T(8,128)(2,1)S(1)}, u32[]{:S(2)}, u32[]{:S(2)}) collective-permute-start(bf16[512,256]{1,0:T(8,128)(2,1)S(1)} %collective-permute-done.25.refs_8_), channel_id=1, source_target_pairs={{0,8},{8,0},{16,24},{24,16},{32,40},{40,32},{48,56},{56,48},{64,72... | collective-permute-start | bytes 786440 | tf_op jit(solution)/shard_map/ppermute | solution.py:88
  109.6 1.6 collective-permute-start.27
  114.8 10.1 %collective-permute-start.28 = (bf16[176,384]{1,0:T(8,128)(2,1)S(1)}, bf16[176,384]{1,0:T(8,128)(2,1)S(1)}, u32[]{:S(2)}, u32[]{:S(2)}) collective-permute-start(bf16[176,384]{1,0:T(8,128)(2,1)S(1)} %get-tuple-element.113), channel_id=1, source_target_pairs={{0,2},{1,3},{2,4},{3,5},{4,6},{5,7},{6,0},{7,1},{8,10},{9,11},{10,... | collective-permute-start | bytes 405512 | tf_op jit(solution)/shard_map/ppermute | solution.py:128
  116.2 9.5 %collective-permute-start.30 = (bf16[176,384]{1,0:T(8,128)(2,1)S(1)}, bf16[176,384]{1,0:T(8,128)(2,1)S(1)}, u32[]{:S(2)}, u32[]{:S(2)}) collective-permute-start(bf16[176,384]{1,0:T(8,128)(2,1)S(1)} %get-tuple-element.115), channel_id=1, source_target_pairs={{0,6},{1,7},{2,0},{3,1},{4,2},{5,3},{6,4},{7,5},{8,14},{9,15},{10,... | collective-permute-start | bytes 405512 | tf_op jit(solution)/shard_map/ppermute | solution.py:128
  118.5 16.1 %copy-start.3 = (s32[2048]{0:T(1024)S(1)}, s32[2048]{0:T(1024)}, u32[]{:S(2)}) copy-start(s32[2048]{0:T(1024)} %param.15) | copy-start | bytes 24580
  125.0 8.4 %collective-permute-start.29 = (bf16[176,256]{1,0:T(8,128)(2,1)S(1)}, bf16[176,256]{1,0:T(8,128)(2,1)S(1)}, u32[]{:S(2)}, u32[]{:S(2)}) collective-permute-start(bf16[176,256]{1,0:T(8,128)(2,1)S(1)} %add_convert_fusion.7), channel_id=1, source_target_pairs={{0,2},{1,3},{2,4},{3,5},{4,6},{5,7},{6,0},{7,1},{8,10},{9,11},{10,... | collective-permute-start | bytes 270344 | tf_op jit(solution)/shard_map/ppermute | solution.py:128
  125.8 7.5 %collective-permute-start.31 = (bf16[176,256]{1,0:T(8,128)(2,1)S(1)}, bf16[176,256]{1,0:T(8,128)(2,1)S(1)}, u32[]{:S(2)}, u32[]{:S(2)}) collective-permute-start(bf16[176,256]{1,0:T(8,128)(2,1)S(1)} %add_convert_fusion.6), channel_id=1, source_target_pairs={{0,6},{1,7},{2,0},{3,1},{4,2},{5,3},{6,4},{7,5},{8,14},{9,15},{10,... | collective-permute-start | bytes 270344 | tf_op jit(solution)/shard_map/ppermute | solution.py:128
  129.0 5.2 %collective-permute-start.32 = (bf16[176,256]{1,0:T(8,128)(2,1)S(1)}, bf16[176,256]{1,0:T(8,128)(2,1)S(1)}, u32[]{:S(2)}, u32[]{:S(2)}) collective-permute-start(bf16[176,256]{1,0:T(8,128)(2,1)S(1)} %add_convert_fusion.5), channel_id=1, source_target_pairs={{0,1},{1,2},{2,3},{3,4},{4,5},{5,6},{6,7},{7,0},{8,9},{9,10},{10,1... | collective-permute-start | bytes 270344 | tf_op jit(solution)/shard_map/ppermute | solution.py:128
  129.1 5.5 %collective-permute-start.33 = (bf16[176,256]{1,0:T(8,128)(2,1)S(1)}, bf16[176,256]{1,0:T(8,128)(2,1)S(1)}, u32[]{:S(2)}, u32[]{:S(2)}) collective-permute-start(bf16[176,256]{1,0:T(8,128)(2,1)S(1)} %add_convert_fusion.4), channel_id=1, source_target_pairs={{0,7},{1,0},{2,1},{3,2},{4,3},{5,4},{6,5},{7,6},{8,15},{9,8},{10,9... | collective-permute-start | bytes 270344 | tf_op jit(solution)/shard_map/ppermute | solution.py:128
  135.4 5.4 %collective-permute-start.35 = (bf16[176,256]{1,0:T(8,128)(2,1)S(1)}, bf16[176,256]{1,0:T(8,128)(2,1)S(1)}, u32[]{:S(2)}, u32[]{:S(2)}) collective-permute-start(bf16[176,256]{1,0:T(8,128)(2,1)S(1)} %get-tuple-element.126.refs_5_), channel_id=1, source_target_pairs={{0,6},{1,7},{2,0},{3,1},{4,2},{5,3},{6,4},{7,5},{8,14},{9,15},{10,... | collective-permute-start | bytes 270344 | tf_op jit(solution)/shard_map/ppermute | solution.py:128
  137.5 5.5 %collective-permute-start.34 = (bf16[176,256]{1,0:T(8,128)(2,1)S(1)}, bf16[176,256]{1,0:T(8,128)(2,1)S(1)}, u32[]{:S(2)}, u32[]{:S(2)}) collective-permute-start(bf16[176,256]{1,0:T(8,128)(2,1)S(1)} %get-tuple-element.126.refs_5_), channel_id=1, source_target_pairs={{0,7},{1,0},{2,1},{3,2},{4,3},{5,4},{6,5},{7,6},{8,15},{9,8},{10,9... | collective-permute-start | bytes 270344 | tf_op jit(solution)/shard_map/ppermute | solution.py:128
  137.5 6.3 %collective-permute-start.36 = (bf16[176,256]{1,0:T(8,128)(2,1)S(1)}, bf16[176,256]{1,0:T(8,128)(2,1)S(1)}, u32[]{:S(2)}, u32[]{:S(2)}) collective-permute-start(bf16[176,256]{1,0:T(8,128)(2,1)S(1)} %get-tuple-element.126.refs_5_), channel_id=1, source_target_pairs={{0,2},{1,3},{2,4},{3,5},{4,6},{5,7},{6,0},{7,1},{8,10},{9,11},{10,... | collective-permute-start | bytes 270344 | tf_op jit(solution)/shard_map/ppermute | solution.py:128
  139.5 5.7 %collective-permute-start.37 = (bf16[176,256]{1,0:T(8,128)(2,1)S(1)}, bf16[176,256]{1,0:T(8,128)(2,1)S(1)}, u32[]{:S(2)}, u32[]{:S(2)}) collective-permute-start(bf16[176,256]{1,0:T(8,128)(2,1)S(1)} %get-tuple-element.126.refs_5_), channel_id=1, source_target_pairs={{0,1},{1,2},{2,3},{3,4},{4,5},{5,6},{6,7},{7,0},{8,9},{9,10},{10,1... | collective-permute-start | bytes 270344 | tf_op jit(solution)/shard_map/ppermute | solution.py:128
  143.0 6.2 %collective-permute-start.38 = (bf16[176,384]{1,0:T(8,128)(2,1)S(1)}, bf16[176,384]{1,0:T(8,128)(2,1)S(1)}, u32[]{:S(2)}, u32[]{:S(2)}) collective-permute-start(bf16[176,384]{1,0:T(8,128)(2,1)S(1)} %pad_maximum_fusion), channel_id=1, source_target_pairs={{0,6},{1,7},{2,0},{3,1},{4,2},{5,3},{6,4},{7,5},{8,14},{9,15},{10,... | collective-permute-start | bytes 405512 | tf_op jit(solution)/shard_map/ppermute | solution.py:128
  145.2 6.4 %collective-permute-start.39 = (bf16[176,384]{1,0:T(8,128)(2,1)S(1)}, bf16[176,384]{1,0:T(8,128)(2,1)S(1)}, u32[]{:S(2)}, u32[]{:S(2)}) collective-permute-start(bf16[176,384]{1,0:T(8,128)(2,1)S(1)} %pad_maximum_fusion.1), channel_id=1, source_target_pairs={{0,2},{1,3},{2,4},{3,5},{4,6},{5,7},{6,0},{7,1},{8,10},{9,11},{10,... | collective-permute-start | bytes 405512 | tf_op jit(solution)/shard_map/ppermute | solution.py:128
where the time goes:
time: 204 us; the launch traced here: 203 us
  waiting for transfers between devices  63.8 us (31%)
  starting transfers between devices  56.4 us (28%)
  blocking collectives  42 us (21%)
  Pallas kernels  27.7 us (14%)
  other arithmetic  5.84 us (3%)
  between operations  4.11 us (2%)
  local copies, waits for them, and re-layouts  3.31 us (2%)
    ppermute x22, waiting for transfers between devices, gather_row(): send = lambda v, perm: lax.ppermute(v, 'row', perm)  38 us
    ppermute x18, starting transfers between devices, along_col(): return lax.ppermute(value, 'col', [(i, (i + step) % GZ) for i in range(GZ)])  30.3 us
    ppermute x22, starting transfers between devices, gather_row(): send = lambda v, perm: lax.ppermute(v, 'row', perm)  26.2 us
    ppermute x18, waiting for transfers between devices, along_col(): return lax.ppermute(value, 'col', [(i, (i + step) % GZ) for i in range(GZ)])  25.8 us
    all_to_all x1, blocking collectives, sum_everywhere(): lax.all_to_all(grads.reshape(32, 16, FEAT), 'row', 0, 0, tiled=True)  17.8 us
    all_to_all x1, blocking collectives, sum_everywhere(): lax.all_to_all(jnp.broadcast_to(share, (32, 16, FEAT)), 'row', 0, 0, tile...  13.9 us
    all_to_all x1, blocking collectives, sum_everywhere(): lax.all_to_all(jnp.broadcast_to(share, (GZ, 16, FEAT)), 'col', 0, 0, tile...  10.3 us
    pallas_call x1, Pallas kernels, backward_late(): pl.pallas_call(backward_late_kernel, name='backward_late', out_shape=jax....  8.07 us
  transfers between devices with their start and end apart: 40, of which 26 were waited for; matrix products, arithmetic and copies ran while one was open for 3% of the time, Pallas kernels for 6%

commit v1 on v0

--- a/solution.py
+++ b/solution.py
@@ -84,7 +84,7 @@
     return row_perm(lambda x, y, c: (x, y, 1 - c))
 
 
-def gather_row(own, beside, relay):
+def gather_row(own, beside):
     send = lambda v, perm: lax.ppermute(v, "row", perm)
     line = jnp.concatenate(
         [
@@ -95,19 +95,14 @@
         ],
         0,
     )
-    half = line.shape[0] // 2
     plus = send(line, second_axis(-1))
     minus = send(line, second_axis(1))
-    if relay:
-        late = [send(minus[:half], second_axis(1)), send(plus[half:], second_axis(-1))]
-        line, plus, minus = lax.optimization_barrier((line, plus, minus))
-    else:
-        late = [send(line, second_axis(2))]
-        line, plus = lax.optimization_barrier((line, plus))
+    two = send(line, second_axis(2))
+    line, plus = lax.optimization_barrier((line, plus))
     early = [line, plus, minus]
-    early = early + [send(v, swap_core()) for v in early]
-    late[-1], done = lax.optimization_barrier((late[-1], beside(early)))
-    return early, late + [send(v, swap_core()) for v in late], done
+    swapped = [send(v, swap_core()) for v in early]
+    two, done = lax.optimization_barrier((two, beside(early)))
+    return early, [two] + swapped + [send(two, swap_core())], done
 
 
 def source_slots(col_ids):
@@ -118,10 +113,9 @@
     other = device & 1
     along_first = jnp.where(other == 0, dy, dx)
     along_second = jnp.where(other == 0, dx, dy)
-    swapped = (other ^ me) & 1
-    early = (swapped * 3 + jnp.where(along_second == 3, 2, along_second)) * 4
-    line = jnp.where(along_second == 2, 24 + swapped * 4, early)
-    return (line + along_first) * 2 + (col_ids & 1)
+    line = jnp.where(along_second > 1, 5 - along_second, along_second)
+    line = ((other ^ me) & 1) * 4 + line
+    return (line * 4 + along_first) * 2 + (col_ids & 1)
 
 
 def along_col(value, step):
@@ -564,6 +558,25 @@
     return full.reshape(512, FEAT)
 
 
+def unpack_kernel(grads, grad_one, grad_two_t):
+    grad_one[...] = grads[0:FEAT].astype(F32)
+    grad_two_t[...] = grads[FEAT : FEAT + CPAD].astype(F32)[:CLASSES]
+
+
+def unpack(grads):
+    return pl.pallas_call(
+        unpack_kernel,
+        name="unpack",
+        out_shape=(
+            jax.ShapeDtypeStruct((FEAT, FEAT), F32),
+            jax.ShapeDtypeStruct((CLASSES, FEAT), F32),
+        ),
+        in_specs=[vmem_spec()],
+        out_specs=[vmem_spec()] * 2,
+        compiler_params=params(4),
+    )(grads)
+
+
 def body(features, weight_one, weight_two, adj_tiles, tile_rows, tile_cols, tile_counts, labels):
     z = lax.axis_index("col")
     node_total = ROWS * lax.axis_size("row") * lax.axis_size("col")
@@ -585,7 +598,7 @@
         *ready, tiles = lax.optimization_barrier(ready)
         return (*ready, hold_tiles(tiles, early[0]))
 
-    early, late, done = gather_row(features, prepare, False)
+    early, late, done = gather_row(features, prepare)
     forward, reverse, labels, place, tiles = done
     parts, _ = spread_and_reduce(
         aggregate_early_kernel,
@@ -599,7 +612,7 @@
     )
     agg, weight_one_t, weight_two_t, weight_two = middle(parts, weight_one, second_t)
     early, late, begun = gather_row(
-        agg, functools.partial(early_gates, weight_one_t, weight_two_t), True
+        agg, functools.partial(early_gates, weight_one_t, weight_two_t)
     )
     parts, panel = spread_and_reduce(
         logits_early_kernel,
@@ -617,10 +630,8 @@
     grads = backward_late(
         reverse, tiles, weight_two, total, (*begun[1:], *panel), up, down
     )
-    grads = sum_everywhere(grads)
-    grad_one = grads[:FEAT].astype(F32)
-    grad_two = grads[FEAT : FEAT + CLASSES].astype(F32).T
-    return logits_t.T, grad_one, grad_two
+    grad_one, grad_two_t = unpack(sum_everywhere(grads))
+    return logits_t.T, grad_one, grad_two_t.T
 
 
 def solution(mesh):

time: 204 us -> 204 us (level)
  waiting for transfers between devices: 63.8 us -> 59.3 us
  Pallas kernels: 27.7 us -> 31.5 us
  blocking collectives: 42 us -> 44.6 us
    ppermute x22 -> x20, waiting for transfers between devices: 38 us -> 30.3 us  [gather_row(): send = lambda v, perm: lax.ppermute(v, 'row', perm)]
    ppermute x18, waiting for transfers between devices: 25.8 us -> 29 us  [along_col(): return lax.ppermute(value, 'col', [(i, (i + step) % GZ) for i in range(GZ)])]
    ppermute x18, starting transfers between devices: 30.3 us -> 27.1 us  [along_col(): return lax.ppermute(value, 'col', [(i, (i + step) % GZ) for i in range(GZ)])]
    ppermute x22 -> x20, starting transfers between devices: 26.2 us -> 29.2 us  [gather_row(): send = lambda v, perm: lax.ppermute(v, 'row', perm)]
    pallas_call x2, Pallas kernels: 5.72 us -> 8.73 us  [spread_and_reduce(): pl.pallas_call(early_kernel, name=name + '_early', out_shape=(jax.ShapeDt...]
    pallas_call x1, Pallas kernels: 4.92 us -> 2.45 us  [early_gates(): pl.pallas_call(gates_kernel, name='early_gates', out_shape=(jax.ShapeDtyp...]
  transfers between devices with their start and end apart: 40 -> 38, of which waited for: 26 -> 24; matrix products, arithmetic and copies ran while one was open for 3% -> 3% of each run, Pallas kernels for 6% -> 6%
where the time goes in v1:
time: 204 us; the launch traced here: 203 us
  waiting for transfers between devices  59.3 us (29%)
  starting transfers between devices  56.3 us (28%)
  blocking collectives  44.6 us (22%)
  Pallas kernels  31.5 us (15%)
  other arithmetic  4.34 us (2%)
  between operations  4.12 us (2%)
  local copies, waits for them, and re-layouts  3.27 us (2%)
    ppermute x20, waiting for transfers between devices, gather_row(): send = lambda v, perm: lax.ppermute(v, 'row', perm)  30.3 us
    ppermute x20, starting transfers between devices, gather_row(): send = lambda v, perm: lax.ppermute(v, 'row', perm)  29.2 us
    ppermute x18, waiting for transfers between devices, along_col(): return lax.ppermute(value, 'col', [(i, (i + step) % GZ) for i in range(GZ)])  29 us
    ppermute x18, starting transfers between devices, along_col(): return lax.ppermute(value, 'col', [(i, (i + step) % GZ) for i in range(GZ)])  27.1 us
    all_to_all x1, blocking collectives, sum_everywhere(): lax.all_to_all(grads.reshape(32, 16, FEAT), 'row', 0, 0, tiled=True)  19.1 us
    all_to_all x1, blocking collectives, sum_everywhere(): lax.all_to_all(jnp.broadcast_to(share, (32, 16, FEAT)), 'row', 0, 0, tile...  13.9 us
    all_to_all x1, blocking collectives, sum_everywhere(): lax.all_to_all(jnp.broadcast_to(share, (GZ, 16, FEAT)), 'col', 0, 0, tile...  11.6 us
    pallas_call x2, Pallas kernels, spread_and_reduce(): pl.pallas_call(early_kernel, name=name + '_early', out_shape=(jax.ShapeDt...  8.73 us
  transfers between devices with their start and end apart: 38, of which 24 were waited for; matrix products, arithmetic and copies ran while one was open for 3% of the time, Pallas kernels for 6%

profile of v1, /device:TPU:1, one launch (start us, length us, event | category | flops | bytes accessed | tf_op | source)
XLA Modules:
  0.0 203.4 jit_solution(11339198972744483128)
XLA Ops:
  0.6 3.4 %collective-permute-start = (bf16[256,256]{1,0:T(8,128)(2,1)}, bf16[256,256]{1,0:T(8,128)(2,1)S(1)}, u32[]{:S(2)}, u32[]{:S(2)}) collective-permute-start(bf16[256,256]{1,0:T(8,128)(2,1)} %param.8), channel_id=1, source_target_pairs={{0,48},{8,200},{16,0},{24,216},{32,16},{40,232},{48,32},{56,248},{... | collective-permute-start | bytes 393224 | tf_op jit(solution)/shard_map/ppermute | solution.py:88
  6.1 1.6 collective-permute-done
  7.7 2.0 collective-permute-done.1
  9.7 1.6 collective-permute-done.2
  11.3 2.5 %collective-permute-start.4 = (bf16[1024,256]{1,0:T(8,128)(2,1)S(1)}, bf16[1024,256]{1,0:T(8,128)(2,1)S(1)}, u32[]{:S(2)}, u32[]{:S(2)}) collective-permute-start(bf16[1024,256]{1,0:T(8,128)(2,1)S(1)} %constant_dynamic-update-slice_fusion.after.refs_5_), channel_id=1, source_target_pairs={{0,192},{8,56},{16,208},{24,8},{32,224},{40,24},{48,240},{56,40},{... | collective-permute-start | bytes 1572872 | tf_op jit(solution)/shard_map/ppermute | solution.py:88
  14.6 1.6 collective-permute-start.3
  16.2 9.3 %collective-permute-done.4.refs_6_ = bf16[1024,256]{1,0:T(8,128)(2,1)S(1)} collective-permute-done((bf16[1024,256]{1,0:T(8,128)(2,1)S(1)}, bf16[1024,256]{1,0:T(8,128)(2,1)S(1)}, u32[]{:S(2)}, u32[]{:S(2)}) %collective-permute-start.4) | collective-permute-done | bytes 524320 | tf_op jit(solution)/shard_map/ppermute | solution.py:88
  27.2 3.1 %collective-permute-start.6 = (bf16[1024,256]{1,0:T(8,128)(2,1)S(1)}, bf16[1024,256]{1,0:T(8,128)(2,1)S(1)}, u32[]{:S(2)}, u32[]{:S(2)}) collective-permute-start(bf16[1024,256]{1,0:T(8,128)(2,1)S(1)} %constant_dynamic-update-slice_fusion.after.refs_5_), channel_id=1, source_target_pairs={{0,8},{8,0},{16,24},{24,16},{32,40},{40,32},{48,56},{56,48},{64,72... | collective-permute-start | bytes 1572872 | tf_op jit(solution)/shard_map/ppermute | solution.py:88
  35.3 2.2 %copy-done = bf16[1,1,128,128,128]{4,3,2,1,0:T(8,128)(2,1)S(1)} copy-done((bf16[1,1,128,128,128]{4,3,2,1,0:T(8,128)(2,1)S(1)}, bf16[1,1,128,128,128]{4,3,2,1,0:T(8,128)(2,1)}, u32[]{:S(2)}) %copy-start) | copy-done | bytes 4194328
  38.5 1.4 collective-permute-done.8.refs_11_
  40.7 2.4 %aggregate_early.1 = (bf16[65,128,256]{2,1,0:T(8,128)(2,1)S(1)}, bf16[256,384]{1,0:T(8,128)(2,1)S(1)}, bf16[256,384]{1,0:T(8,128)(2,1)S(1)}) custom-call(s32[208]{0:T(256)S(1)} %get-tuple-element.84.refs_0_, s32[208]{0:T(256)S(1)} %broadcast_add_fusion.1.refs_1_, s32[52]{0:T(128)S(1)} %select_reduce_fusion.6.refs_2_, s32[2]{0:T(128)S(1)} %get-tuple-element.87.refs_3_, ...), custom_call_target="tpu_custom_call" | custom-call | flops 1000000000 | bytes 10000000 | tf_op jit(solution)/shard_map/aggregate_early/pallas_call | solution.py:373
  43.1 2.4 %collective-permute-start.10 = (bf16[256,384]{1,0:T(8,128)(2,1)S(1)}, bf16[256,384]{1,0:T(8,128)(2,1)S(1)}, u32[]{:S(2)}, u32[]{:S(2)}) collective-permute-start(bf16[256,384]{1,0:T(8,128)(2,1)S(1)} %get-tuple-element.94), channel_id=1, source_target_pairs={{0,2},{1,3},{2,4},{3,5},{4,6},{5,7},{6,0},{7,1},{8,10},{9,11},{10,... | collective-permute-start | bytes 589832 | tf_op jit(solution)/shard_map/ppermute | solution.py:122
  45.5 3.8 %collective-permute-start.12 = (bf16[256,384]{1,0:T(8,128)(2,1)S(1)}, bf16[256,384]{1,0:T(8,128)(2,1)S(1)}, u32[]{:S(2)}, u32[]{:S(2)}) collective-permute-start(bf16[256,384]{1,0:T(8,128)(2,1)S(1)} %get-tuple-element.96), channel_id=1, source_target_pairs={{0,6},{1,7},{2,0},{3,1},{4,2},{5,3},{6,4},{7,5},{8,14},{9,15},{10,... | collective-permute-start | bytes 589832 | tf_op jit(solution)/shard_map/ppermute | solution.py:122
  49.3 2.8 %aggregate_late.1 = (f32[256,256]{1,0:T(8,128)S(1)}, f32[256,256]{1,0:T(8,128)S(1)}, f32[256,256]{1,0:T(8,128)S(1)}, f32[256,256]{1,0:T(8,128)S(1)}, f32[256,256]{1,0:T(8,128)S(1)}) custom-call(s32[208]{0:T(256)S(1)} %get-tuple-element.84.refs_0_, s32[208]{0:T(256)S(1)} %broadcast_add_fusion.1.refs_1_, s32[52]{0:T(128)S(1)} %select_reduce_fusion.6.refs_2_, ...), custom_call_target="tpu_custom_call" | custom-call | flops 1000000000 | bytes 10000000 | tf_op jit(solution)/shard_map/aggregate_late/pallas_call | solution.py:383
  52.0 6.2 %collective-permute-done.10 = bf16[256,384]{1,0:T(8,128)(2,1)S(1)} collective-permute-done((bf16[256,384]{1,0:T(8,128)(2,1)S(1)}, bf16[256,384]{1,0:T(8,128)(2,1)S(1)}, u32[]{:S(2)}, u32[]{:S(2)}) %collective-permute-start.10) | collective-permute-done | bytes 196640 | tf_op jit(solution)/shard_map/ppermute | solution.py:122
  59.9 2.4 %collective-permute-start.13 = (bf16[256,256]{1,0:T(8,128)(2,1)S(1)}, bf16[256,256]{1,0:T(8,128)(2,1)S(1)}, u32[]{:S(2)}, u32[]{:S(2)}) collective-permute-start(bf16[256,256]{1,0:T(8,128)(2,1)S(1)} %add_convert_fusion.2), channel_id=1, source_target_pairs={{0,6},{1,7},{2,0},{3,1},{4,2},{5,3},{6,4},{7,5},{8,14},{9,15},{10,... | collective-permute-start | bytes 393224 | tf_op jit(solution)/shard_map/ppermute | solution.py:122
  62.4 1.5 collective-permute-start.15
  63.9 3.0 %collective-permute-done.11.refs_1_ = bf16[256,256]{1,0:T(8,128)(2,1)S(1)} collective-permute-done((bf16[256,256]{1,0:T(8,128)(2,1)S(1)}, bf16[256,256]{1,0:T(8,128)(2,1)S(1)}, u32[]{:S(2)}, u32[]{:S(2)}) %collective-permute-start.11) | collective-permute-done | bytes 131104 | tf_op jit(solution)/shard_map/ppermute | solution.py:122
  66.8 1.8 collective-permute-done.14.refs_3_
  68.6 4.5 %collective-permute-done.15.refs_4_ = bf16[256,256]{1,0:T(8,128)(2,1)S(1)} collective-permute-done((bf16[256,256]{1,0:T(8,128)(2,1)S(1)}, bf16[256,256]{1,0:T(8,128)(2,1)S(1)}, u32[]{:S(2)}, u32[]{:S(2)}) %collective-permute-start.15) | collective-permute-done | bytes 131104 | tf_op jit(solution)/shard_map/ppermute | solution.py:122
  73.4 2.6 %collective-permute-start.16 = (bf16[256,256]{1,0:T(8,128)(2,1)S(1)}, bf16[256,256]{1,0:T(8,128)(2,1)S(1)}, u32[]{:S(2)}, u32[]{:S(2)}) collective-permute-start(bf16[256,256]{1,0:T(8,128)(2,1)S(1)} %get-tuple-element.101), channel_id=1, source_target_pairs={{0,48},{8,200},{16,0},{24,216},{32,16},{40,232},{48,32},{56,248},{... | collective-permute-start | bytes 393224 | tf_op jit(solution)/shard_map/ppermute | solution.py:88
  76.0 1.3 collective-permute-start.17
  78.0 3.7 %collective-permute-done.17 = bf16[256,256]{1,0:T(8,128)(2,1)S(1)} collective-permute-done((bf16[256,256]{1,0:T(8,128)(2,1)S(1)}, bf16[256,256]{1,0:T(8,128)(2,1)S(1)}, u32[]{:S(2)}, u32[]{:S(2)}) %collective-permute-start.17) | collective-permute-done | bytes 131104 | tf_op jit(solution)/shard_map/ppermute | solution.py:88
  82.4 1.4 collective-permute-start.20
  85.1 5.8 %collective-permute-done.20.rest_1_ = bf16[1024,256]{1,0:T(8,128)(2,1)S(1)} collective-permute-done((bf16[1024,256]{1,0:T(8,128)(2,1)S(1)}, bf16[1024,256]{1,0:T(8,128)(2,1)S(1)}, u32[]{:S(2)}, u32[]{:S(2)}) %collective-permute-start.20) | collective-permute-done | bytes 524320 | tf_op jit(solution)/shard_map/ppermute | solution.py:88
  90.9 7.2 %collective-permute-start.22 = (bf16[1024,256]{1,0:T(8,128)(2,1)S(1)}, bf16[1024,256]{1,0:T(8,128)(2,1)S(1)}, u32[]{:S(2)}, u32[]{:S(2)}) collective-permute-start(bf16[1024,256]{1,0:T(8,128)(2,1)S(1)} %constant_dynamic-update-slice_fusion.4.rest_0_), channel_id=1, source_target_pairs={{0,8},{8,0},{16,24},{24,16},{32,40},{40,32},{48,56},{56,48},{64,72... | collective-permute-start | bytes 1572872 | tf_op jit(solution)/shard_map/ppermute | solution.py:88
  99.0 2.8 %collective-permute-start.24 = (bf16[1024,256]{1,0:T(8,128)(2,1)S(1)}, bf16[1024,256]{1,0:T(8,128)(2,1)S(1)}, u32[]{:S(2)}, u32[]{:S(2)}) collective-permute-start(bf16[1024,256]{1,0:T(8,128)(2,1)S(1)} %collective-permute-done.21.rest_2_), channel_id=1, source_target_pairs={{0,8},{8,0},{16,24},{24,16},{32,40},{40,32},{48,56},{56,48},{64,72... | collective-permute-start | bytes 1572872 | tf_op jit(solution)/shard_map/ppermute | solution.py:88
  101.7 2.4 %early_gates.1 = (bf16[24,176,128]{2,1,0:T(8,128)(2,1)S(1)}, bf16[3072,256]{1,0:T(8,128)(2,1)S(1)}, bf16[256,3072]{1,0:T(8,128)(2,1)S(1)}, bf16[256,3072]{1,0:T(8,128)(2,1)S(1)}) custom-call(bf16[256,256]{1,0:T(8,128)(2,1)S(1)} %get-tuple-element.99.weight_one_t.refs_5_, bf16[176,256]{1,0:T(8,128)(2,1)S(1)} %get-tuple-element.100.weight_two_t.refs_6_, ...), custom_call_target="tpu_custom_call" | custom-call | flops 1000 | bytes 1000 | tf_op jit(solution)/shard_map/early_gates/pallas_call | solution.py:328
  104.3 1.9 collective-permute-done.25.refs_12_
  106.2 6.3 %partial_logits_early.1 = (bf16[65,176,128]{2,1,0:T(8,128)(2,1)S(1)}, bf16[176,384]{1,0:T(8,128)(2,1)S(1)}, bf16[176,384]{1,0:T(8,128)(2,1)S(1)}, bf16[5120,256]...) custom-call(s32[208]{0:T(256)S(1)} %get-tuple-element.84.refs_0_, ...), custom_call_target="tpu_custom_call" | custom-call | flops 1000000000 | bytes 10000000 | tf_op jit(solution)/shard_map/partial_logits_early/pallas_call | solution.py:373
  112.5 2.0 collective-permute-start.26
  114.5 1.7 collective-permute-start.28
  116.2 2.9 %partial_logits_late.1 = (f32[176,256]{1,0:T(8,128)S(1)}, f32[176,256]{1,0:T(8,128)S(1)}, f32[176,256]{1,0:T(8,128)S(1)}, f32[176,256]{1,0:T(8,128)S(1)}, f32[176,256]{1,0:T(8,128)S(1)}) custom-call(s32[208]{0:T(256)S(1)} %get-tuple-element.84.refs_0_, s32[208]{0:T(256)S(1)} %broadcast_add_fusion.1.refs_1_, s32[52]{0:T(128)S(1)} %select_reduce_fusion.6.refs_2_, ...), custom_call_target="tpu_custom_call" | custom-call | flops 1000000000 | bytes 10000000 | tf_op jit(solution)/shard_map/partial_logits_late/pallas_call | solution.py:383
  119.1 4.0 %collective-permute-done.26 = bf16[176,384]{1,0:T(8,128)(2,1)S(1)} collective-permute-done((bf16[176,384]{1,0:T(8,128)(2,1)S(1)}, bf16[176,384]{1,0:T(8,128)(2,1)S(1)}, u32[]{:S(2)}, u32[]{:S(2)}) %collective-permute-start.26) | collective-permute-done | bytes 135200 | tf_op jit(solution)/shard_map/ppermute | solution.py:122
  123.2 2.1 %collective-permute-start.30 = (bf16[176,256]{1,0:T(8,128)(2,1)S(1)}, bf16[176,256]{1,0:T(8,128)(2,1)S(1)}, u32[]{:S(2)}, u32[]{:S(2)}) collective-permute-start(bf16[176,256]{1,0:T(8,128)(2,1)S(1)} %add_convert_fusion.5), channel_id=1, source_target_pairs={{0,1},{1,2},{2,3},{3,4},{4,5},{5,6},{6,7},{7,0},{8,9},{9,10},{10,1... | collective-permute-start | bytes 270344 | tf_op jit(solution)/shard_map/ppermute | solution.py:122
  125.3 1.9 collective-permute-start.29
  127.2 1.5 collective-permute-start.31
  128.7 1.9 collective-permute-done.27.refs_1_
  130.6 1.6 collective-permute-done.29.refs_2_
  132.2 1.3 collective-permute-done.31.refs_4_
  137.4 1.2 collective-permute-start.34
  138.5 3.0 %collective-permute-done.32.refs_6_ = bf16[176,256]{1,0:T(8,128)(2,1)S(1)} collective-permute-done((bf16[176,256]{1,0:T(8,128)(2,1)S(1)}, bf16[176,256]{1,0:T(8,128)(2,1)S(1)}, u32[]{:S(2)}, u32[]{:S(2)}) %collective-permute-start.32) | collective-permute-done | bytes 90144 | tf_op jit(solution)/shard_map/ppermute | solution.py:122
  143.2 1.6 collective-permute-start.37
  144.8 4.3 %backward_early.1.refs_6_ = f32[64,176,128]{2,1,0:T(8,128)S(1)} custom-call(s32[272]{0:T(512)S(1)} %get-tuple-element.121.refs_0_, s32[272]{0:T(512)S(1)} %broadcast_add_fusion.refs_1_, s32[136]{0:T(256)S(1)} %select_reduce_fusion.4.refs_2_, s32[2]{0:T(128)S(1)} %get-tuple-element.124.refs_3_, bf16[128,128,128]{2,1,0:T(8,128)(2,1)S(1)} %hold_tiles.1.refs_4_, ...), custom_call_target="tpu_custom_call" | custom-call | flops 1000 | bytes 1000 | tf_op jit(solution)/shard_map/backward_early/pallas_call | solution.py:481
  149.6 8.3 %backward_late.1 = bf16[512,256]{1,0:T(8,128)(2,1)S(1)} custom-call(s32[272]{0:T(512)S(1)} %get-tuple-element.121.refs_0_, s32[272]{0:T(512)S(1)} %broadcast_add_fusion.refs_1_, s32[136]{0:T(256)S(1)} %select_reduce_fusion.4.refs_2_, s32[2]{0:T(128)S(1)} %get-tuple-element.124.refs_3_, bf16[128,128,128]{2,1,0:T(8,128)(2,1)S(1)} %hold_tiles.1.refs_4_, ...), custom_call_target="tpu_custom_call" | custom-call | flops 5000000000 | bytes 20000000 | tf_op jit(solution)/shard_map/backward_late/pallas_call | solution.py:533
  157.9 19.1 %all_to_all.15 = bf16[32,16,256]{2,1,0:T(8,128)(2,1)S(1)} all-to-all(bf16[32,16,256]{2,1,0:T(8,128)(2,1)S(1)} %bitcast.14), channel_id=1, replica_groups=mesh['row'=32,'col'=8] {'row'}, dimensions={0} | all-to-all | bytes 524288 | tf_op jit(solution)/shard_map/all_to_all | solution.py:551
  177.1 11.6 %all_to_all.16 = bf16[8,16,256]{2,1,0:T(8,128)(2,1)S(1)} all-to-all(bf16[8,16,256]{2,1,0:T(8,128)(2,1)S(1)} %broadcast_in_dim.222), channel_id=1, replica_groups=mesh['row'=32,'col'=8] {'col'}, dimensions={0} | all-to-all | bytes 131072 | tf_op jit(solution)/shard_map/all_to_all | solution.py:553
  188.7 13.9 %all_to_all.17 = bf16[32,16,256]{2,1,0:T(8,128)(2,1)S(1)} all-to-all(bf16[32,16,256]{2,1,0:T(8,128)(2,1)S(1)} %broadcast_in_dim.223), channel_id=1, replica_groups=mesh['row'=32,'col'=8] {'row'}, dimensions={0} | all-to-all | bytes 524288 | tf_op jit(solution)/shard_map/all_to_all | solution.py:557
  (100 shorter events, 20.8 us)
Async XLA Ops:
  0.6 7.1 %collective-permute-start = (bf16[256,256]{1,0:T(8,128)(2,1)}, bf16[256,256]{1,0:T(8,128)(2,1)S(1)}, u32[]{:S(2)}, u32[]{:S(2)}) collective-permute-start(bf16[256,256]{1,0:T(8,128)(2,1)} %param.8), channel_id=1, source_target_pairs={{0,48},{8,200},{16,0},{24,216},{32,16},{40,232},{48,32},{56,248},{... | collective-permute-start | bytes 393224 | tf_op jit(solution)/shard_map/ppermute | solution.py:88
  4.0 5.6 %collective-permute-start.1 = (bf16[256,256]{1,0:T(8,128)(2,1)}, bf16[256,256]{1,0:T(8,128)(2,1)S(1)}, u32[]{:S(2)}, u32[]{:S(2)}) collective-permute-start(bf16[256,256]{1,0:T(8,128)(2,1)} %param.8), channel_id=1, source_target_pairs={{0,32},{8,136},{16,48},{24,152},{32,0},{40,168},{48,16},{56,184},{... | collective-permute-start | bytes 393224 | tf_op jit(solution)/shard_map/ppermute | solution.py:88
  4.5 6.7 %collective-permute-start.2 = (bf16[256,256]{1,0:T(8,128)(2,1)}, bf16[256,256]{1,0:T(8,128)(2,1)S(1)}, u32[]{:S(2)}, u32[]{:S(2)}) collective-permute-start(bf16[256,256]{1,0:T(8,128)(2,1)} %param.8), channel_id=1, source_target_pairs={{0,16},{8,72},{16,32},{24,88},{32,48},{40,104},{48,0},{56,120},{64... | collective-permute-start | bytes 393224 | tf_op jit(solution)/shard_map/ppermute | solution.py:88
  11.3 14.3 %collective-permute-start.4 = (bf16[1024,256]{1,0:T(8,128)(2,1)S(1)}, bf16[1024,256]{1,0:T(8,128)(2,1)S(1)}, u32[]{:S(2)}, u32[]{:S(2)}) collective-permute-start(bf16[1024,256]{1,0:T(8,128)(2,1)S(1)} %constant_dynamic-update-slice_fusion.after.refs_5_), channel_id=1, source_target_pairs={{0,192},{8,56},{16,208},{24,8},{32,224},{40,24},{48,240},{56,40},{... | collective-permute-start | bytes 1572872 | tf_op jit(solution)/shard_map/ppermute | solution.py:88
  14.5 23.3 %collective-permute-start.5 = (bf16[1024,256]{1,0:T(8,128)(2,1)S(1)}, bf16[1024,256]{1,0:T(8,128)(2,1)S(1)}, u32[]{:S(2)}, u32[]{:S(2)}) collective-permute-start(bf16[1024,256]{1,0:T(8,128)(2,1)S(1)} %constant_dynamic-update-slice_fusion.after.refs_5_), channel_id=1, source_target_pairs={{0,64},{8,24},{16,80},{24,40},{32,96},{40,56},{48,112},{56,8},{64,... | collective-permute-start | bytes 1572872 | tf_op jit(solution)/shard_map/ppermute | solution.py:88
  14.6 23.8 %collective-permute-start.3 = (bf16[1024,256]{1,0:T(8,128)(2,1)S(1)}, bf16[1024,256]{1,0:T(8,128)(2,1)S(1)}, u32[]{:S(2)}, u32[]{:S(2)}) collective-permute-start(bf16[1024,256]{1,0:T(8,128)(2,1)S(1)} %constant_dynamic-update-slice_fusion.after.refs_5_), channel_id=1, source_target_pairs={{0,128},{8,40},{16,144},{24,56},{32,160},{40,8},{48,176},{56,24},{... | collective-permute-start | bytes 1572872 | tf_op jit(solution)/shard_map/ppermute | solution.py:88
  27.2 12.7 %collective-permute-start.6 = (bf16[1024,256]{1,0:T(8,128)(2,1)S(1)}, bf16[1024,256]{1,0:T(8,128)(2,1)S(1)}, u32[]{:S(2)}, u32[]{:S(2)}) collective-permute-start(bf16[1024,256]{1,0:T(8,128)(2,1)S(1)} %constant_dynamic-update-slice_fusion.after.refs_5_), channel_id=1, source_target_pairs={{0,8},{8,0},{16,24},{24,16},{32,40},{40,32},{48,56},{56,48},{64,72... | collective-permute-start | bytes 1572872 | tf_op jit(solution)/shard_map/ppermute | solution.py:88
  35.2 4.7 %collective-permute-start.7 = (bf16[1024,256]{1,0:T(8,128)(2,1)S(1)}, bf16[1024,256]{1,0:T(8,128)(2,1)S(1)}, u32[]{:S(2)}, u32[]{:S(2)}) collective-permute-start(bf16[1024,256]{1,0:T(8,128)(2,1)S(1)} %collective-permute-done.4.refs_6_), channel_id=1, source_target_pairs={{0,8},{8,0},{16,24},{24,16},{32,40},{40,32},{48,56},{56,48},{64,72... | collective-permute-start | bytes 1572872 | tf_op jit(solution)/shard_map/ppermute | solution.py:88
  35.3 2.2 %copy-start = (bf16[1,1,128,128,128]{4,3,2,1,0:T(8,128)(2,1)S(1)}, bf16[1,1,128,128,128]{4,3,2,1,0:T(8,128)(2,1)}, u32[]{:S(2)}) copy-start(bf16[1,1,128,128,128]{4,3,2,1,0:T(8,128)(2,1)} %param.11) | copy-start | bytes 12582916
  37.8 2.1 %collective-permute-start.8 = (bf16[1024,256]{1,0:T(8,128)(2,1)S(1)}, bf16[1024,256]{1,0:T(8,128)(2,1)S(1)}, u32[]{:S(2)}, u32[]{:S(2)}) collective-permute-start(bf16[1024,256]{1,0:T(8,128)(2,1)S(1)} %collective-permute-done.5.refs_7_), channel_id=1, source_target_pairs={{0,8},{8,0},{16,24},{24,16},{32,40},{40,32},{48,56},{56,48},{64,72... | collective-permute-start | bytes 1572872 | tf_op jit(solution)/shard_map/ppermute | solution.py:88
  38.4 2.3 %collective-permute-start.9 = (bf16[1024,256]{1,0:T(8,128)(2,1)S(1)}, bf16[1024,256]{1,0:T(8,128)(2,1)S(1)}, u32[]{:S(2)}, u32[]{:S(2)}) collective-permute-start(bf16[1024,256]{1,0:T(8,128)(2,1)S(1)} %collective-permute-done.3.refs_8_), channel_id=1, source_target_pairs={{0,8},{8,0},{16,24},{24,16},{32,40},{40,32},{48,56},{56,48},{64,72... | collective-permute-start | bytes 1572872 | tf_op jit(solution)/shard_map/ppermute | solution.py:88
  43.1 15.1 %collective-permute-start.10 = (bf16[256,384]{1,0:T(8,128)(2,1)S(1)}, bf16[256,384]{1,0:T(8,128)(2,1)S(1)}, u32[]{:S(2)}, u32[]{:S(2)}) collective-permute-start(bf16[256,384]{1,0:T(8,128)(2,1)S(1)} %get-tuple-element.94), channel_id=1, source_target_pairs={{0,2},{1,3},{2,4},{3,5},{4,6},{5,7},{6,0},{7,1},{8,10},{9,11},{10,... | collective-permute-start | bytes 589832 | tf_op jit(solution)/shard_map/ppermute | solution.py:122
  45.5 14.4 %collective-permute-start.12 = (bf16[256,384]{1,0:T(8,128)(2,1)S(1)}, bf16[256,384]{1,0:T(8,128)(2,1)S(1)}, u32[]{:S(2)}, u32[]{:S(2)}) collective-permute-start(bf16[256,384]{1,0:T(8,128)(2,1)S(1)} %get-tuple-element.96), channel_id=1, source_target_pairs={{0,6},{1,7},{2,0},{3,1},{4,2},{5,3},{6,4},{7,5},{8,14},{9,15},{10,... | collective-permute-start | bytes 589832 | tf_op jit(solution)/shard_map/ppermute | solution.py:122
  49.3 23.9 %copy-start.1 = (bf16[256,256]{1,0:T(8,128)(2,1)S(1)}, bf16[256,256]{1,0:T(8,128)(2,1)}, u32[]{:S(2)}) copy-start(bf16[256,256]{1,0:T(8,128)(2,1)} %refs_5_.1) | copy-start | bytes 393220
  49.3 23.9 %copy-start.2 = (bf16[256,172]{0,1:T(8,128)(2,1)S(1)}, bf16[256,172]{0,1:T(8,128)(2,1)}, u32[]{:S(2)}) copy-start(bf16[256,172]{0,1:T(8,128)(2,1)} %param.10) | copy-start | bytes 264196
  58.2 8.6 %collective-permute-start.11 = (bf16[256,256]{1,0:T(8,128)(2,1)S(1)}, bf16[256,256]{1,0:T(8,128)(2,1)S(1)}, u32[]{:S(2)}, u32[]{:S(2)}) collective-permute-start(bf16[256,256]{1,0:T(8,128)(2,1)S(1)} %add_convert_fusion.3), channel_id=1, source_target_pairs={{0,2},{1,3},{2,4},{3,5},{4,6},{5,7},{6,0},{7,1},{8,10},{9,11},{10,... | collective-permute-start | bytes 393224 | tf_op jit(solution)/shard_map/ppermute | solution.py:122
  59.0 9.6 %collective-permute-start.14 = (bf16[256,256]{1,0:T(8,128)(2,1)S(1)}, bf16[256,256]{1,0:T(8,128)(2,1)S(1)}, u32[]{:S(2)}, u32[]{:S(2)}) collective-permute-start(bf16[256,256]{1,0:T(8,128)(2,1)S(1)} %add_convert_fusion.1), channel_id=1, source_target_pairs={{0,1},{1,2},{2,3},{3,4},{4,5},{5,6},{6,7},{7,0},{8,9},{9,10},{10,1... | collective-permute-start | bytes 393224 | tf_op jit(solution)/shard_map/ppermute | solution.py:122
  59.9 8.8 %collective-permute-start.13 = (bf16[256,256]{1,0:T(8,128)(2,1)S(1)}, bf16[256,256]{1,0:T(8,128)(2,1)S(1)}, u32[]{:S(2)}, u32[]{:S(2)}) collective-permute-start(bf16[256,256]{1,0:T(8,128)(2,1)S(1)} %add_convert_fusion.2), channel_id=1, source_target_pairs={{0,6},{1,7},{2,0},{3,1},{4,2},{5,3},{6,4},{7,5},{8,14},{9,15},{10,... | collective-permute-start | bytes 393224 | tf_op jit(solution)/shard_map/ppermute | solution.py:122
  62.4 10.8 %collective-permute-start.15 = (bf16[256,256]{1,0:T(8,128)(2,1)S(1)}, bf16[256,256]{1,0:T(8,128)(2,1)S(1)}, u32[]{:S(2)}, u32[]{:S(2)}) collective-permute-start(bf16[256,256]{1,0:T(8,128)(2,1)S(1)} %add_convert_fusion), channel_id=1, source_target_pairs={{0,7},{1,0},{2,1},{3,2},{4,3},{5,4},{6,5},{7,6},{8,15},{9,8},{10,9... | collective-permute-start | bytes 393224 | tf_op jit(solution)/shard_map/ppermute | solution.py:122
  73.4 4.6 %collective-permute-start.16 = (bf16[256,256]{1,0:T(8,128)(2,1)S(1)}, bf16[256,256]{1,0:T(8,128)(2,1)S(1)}, u32[]{:S(2)}, u32[]{:S(2)}) collective-permute-start(bf16[256,256]{1,0:T(8,128)(2,1)S(1)} %get-tuple-element.101), channel_id=1, source_target_pairs={{0,48},{8,200},{16,0},{24,216},{32,16},{40,232},{48,32},{56,248},{... | collective-permute-start | bytes 393224 | tf_op jit(solution)/shard_map/ppermute | solution.py:88
  76.0 6.4 %collective-permute-start.18 = (bf16[256,256]{1,0:T(8,128)(2,1)S(1)}, bf16[256,256]{1,0:T(8,128)(2,1)S(1)}, u32[]{:S(2)}, u32[]{:S(2)}) collective-permute-start(bf16[256,256]{1,0:T(8,128)(2,1)S(1)} %get-tuple-element.101), channel_id=1, source_target_pairs={{0,16},{8,72},{16,32},{24,88},{32,48},{40,104},{48,0},{56,120},{64... | collective-permute-start | bytes 393224 | tf_op jit(solution)/shard_map/ppermute | solution.py:88
  76.0 5.7 %collective-permute-start.17 = (bf16[256,256]{1,0:T(8,128)(2,1)S(1)}, bf16[256,256]{1,0:T(8,128)(2,1)S(1)}, u32[]{:S(2)}, u32[]{:S(2)}) collective-permute-start(bf16[256,256]{1,0:T(8,128)(2,1)S(1)} %get-tuple-element.101), channel_id=1, source_target_pairs={{0,32},{8,136},{16,48},{24,152},{32,0},{40,168},{48,16},{56,184},{... | collective-permute-start | bytes 393224 | tf_op jit(solution)/shard_map/ppermute | solution.py:88
  82.4 8.4 %collective-permute-start.20 = (bf16[1024,256]{1,0:T(8,128)(2,1)S(1)}, bf16[1024,256]{1,0:T(8,128)(2,1)S(1)}, u32[]{:S(2)}, u32[]{:S(2)}) collective-permute-start(bf16[1024,256]{1,0:T(8,128)(2,1)S(1)} %constant_dynamic-update-slice_fusion.4.rest_0_), channel_id=1, source_target_pairs={{0,192},{8,56},{16,208},{24,8},{32,224},{40,24},{48,240},{56,40},{... | collective-permute-start | bytes 1572872 | tf_op jit(solution)/shard_map/ppermute | solution.py:88
  83.8 15.2 %collective-permute-start.21 = (bf16[1024,256]{1,0:T(8,128)(2,1)S(1)}, bf16[1024,256]{1,0:T(8,128)(2,1)S(1)}, u32[]{:S(2)}, u32[]{:S(2)}) collective-permute-start(bf16[1024,256]{1,0:T(8,128)(2,1)S(1)} %constant_dynamic-update-slice_fusion.4.rest_0_), channel_id=1, source_target_pairs={{0,64},{8,24},{16,80},{24,40},{32,96},{40,56},{48,112},{56,8},{64,... | collective-permute-start | bytes 1572872 | tf_op jit(solution)/shard_map/ppermute | solution.py:88
  84.0 20.2 %collective-permute-start.19 = (bf16[1024,256]{1,0:T(8,128)(2,1)S(1)}, bf16[1024,256]{1,0:T(8,128)(2,1)S(1)}, u32[]{:S(2)}, u32[]{:S(2)}) collective-permute-start(bf16[1024,256]{1,0:T(8,128)(2,1)S(1)} %constant_dynamic-update-slice_fusion.4.rest_0_), channel_id=1, source_target_pairs={{0,128},{8,40},{16,144},{24,56},{32,160},{40,8},{48,176},{56,24},{... | collective-permute-start | bytes 1572872 | tf_op jit(solution)/shard_map/ppermute | solution.py:88
  90.9 13.5 %collective-permute-start.22 = (bf16[1024,256]{1,0:T(8,128)(2,1)S(1)}, bf16[1024,256]{1,0:T(8,128)(2,1)S(1)}, u32[]{:S(2)}, u32[]{:S(2)}) collective-permute-start(bf16[1024,256]{1,0:T(8,128)(2,1)S(1)} %constant_dynamic-update-slice_fusion.4.rest_0_), channel_id=1, source_target_pairs={{0,8},{8,0},{16,24},{24,16},{32,40},{40,32},{48,56},{56,48},{64,72... | collective-permute-start | bytes 1572872 | tf_op jit(solution)/shard_map/ppermute | solution.py:88
  98.0 6.3 %collective-permute-start.23 = (bf16[1024,256]{1,0:T(8,128)(2,1)S(1)}, bf16[1024,256]{1,0:T(8,128)(2,1)S(1)}, u32[]{:S(2)}, u32[]{:S(2)}) collective-permute-start(bf16[1024,256]{1,0:T(8,128)(2,1)S(1)} %collective-permute-done.20.rest_1_), channel_id=1, source_target_pairs={{0,8},{8,0},{16,24},{24,16},{32,40},{40,32},{48,56},{56,48},{64,72... | collective-permute-start | bytes 1572872 | tf_op jit(solution)/shard_map/ppermute | solution.py:88
  99.0 5.3 %collective-permute-start.24 = (bf16[1024,256]{1,0:T(8,128)(2,1)S(1)}, bf16[1024,256]{1,0:T(8,128)(2,1)S(1)}, u32[]{:S(2)}, u32[]{:S(2)}) collective-permute-start(bf16[1024,256]{1,0:T(8,128)(2,1)S(1)} %collective-permute-done.21.rest_2_), channel_id=1, source_target_pairs={{0,8},{8,0},{16,24},{24,16},{32,40},{40,32},{48,56},{56,48},{64,72... | collective-permute-start | bytes 1572872 | tf_op jit(solution)/shard_map/ppermute | solution.py:88
  104.2 2.0 collective-permute-start.25
  112.5 10.5 %collective-permute-start.26 = (bf16[176,384]{1,0:T(8,128)(2,1)S(1)}, bf16[176,384]{1,0:T(8,128)(2,1)S(1)}, u32[]{:S(2)}, u32[]{:S(2)}) collective-permute-start(bf16[176,384]{1,0:T(8,128)(2,1)S(1)} %get-tuple-element.113), channel_id=1, source_target_pairs={{0,2},{1,3},{2,4},{3,5},{4,6},{5,7},{6,0},{7,1},{8,10},{9,11},{10,... | collective-permute-start | bytes 405512 | tf_op jit(solution)/shard_map/ppermute | solution.py:122
  114.5 10.8 %collective-permute-start.28 = (bf16[176,384]{1,0:T(8,128)(2,1)S(1)}, bf16[176,384]{1,0:T(8,128)(2,1)S(1)}, u32[]{:S(2)}, u32[]{:S(2)}) collective-permute-start(bf16[176,384]{1,0:T(8,128)(2,1)S(1)} %get-tuple-element.115), channel_id=1, source_target_pairs={{0,6},{1,7},{2,0},{3,1},{4,2},{5,3},{6,4},{7,5},{8,14},{9,15},{10,... | collective-permute-start | bytes 405512 | tf_op jit(solution)/shard_map/ppermute | solution.py:122
  116.2 17.3 %copy-start.3 = (s32[2048]{0:T(1024)S(1)}, s32[2048]{0:T(1024)}, u32[]{:S(2)}) copy-start(s32[2048]{0:T(1024)} %param.15) | copy-start | bytes 24580
  123.1 7.5 %collective-permute-start.27 = (bf16[176,256]{1,0:T(8,128)(2,1)S(1)}, bf16[176,256]{1,0:T(8,128)(2,1)S(1)}, u32[]{:S(2)}, u32[]{:S(2)}) collective-permute-start(bf16[176,256]{1,0:T(8,128)(2,1)S(1)} %add_convert_fusion.7), channel_id=1, source_target_pairs={{0,2},{1,3},{2,4},{3,5},{4,6},{5,7},{6,0},{7,1},{8,10},{9,11},{10,... | collective-permute-start | bytes 270344 | tf_op jit(solution)/shard_map/ppermute | solution.py:122
  123.2 7.4 %collective-permute-start.30 = (bf16[176,256]{1,0:T(8,128)(2,1)S(1)}, bf16[176,256]{1,0:T(8,128)(2,1)S(1)}, u32[]{:S(2)}, u32[]{:S(2)}) collective-permute-start(bf16[176,256]{1,0:T(8,128)(2,1)S(1)} %add_convert_fusion.5), channel_id=1, source_target_pairs={{0,1},{1,2},{2,3},{3,4},{4,5},{5,6},{6,7},{7,0},{8,9},{9,10},{10,1... | collective-permute-start | bytes 270344 | tf_op jit(solution)/shard_map/ppermute | solution.py:122
  125.3 6.9 %collective-permute-start.29 = (bf16[176,256]{1,0:T(8,128)(2,1)S(1)}, bf16[176,256]{1,0:T(8,128)(2,1)S(1)}, u32[]{:S(2)}, u32[]{:S(2)}) collective-permute-start(bf16[176,256]{1,0:T(8,128)(2,1)S(1)} %add_convert_fusion.6), channel_id=1, source_target_pairs={{0,6},{1,7},{2,0},{3,1},{4,2},{5,3},{6,4},{7,5},{8,14},{9,15},{10,... | collective-permute-start | bytes 270344 | tf_op jit(solution)/shard_map/ppermute | solution.py:122
  127.2 6.2 %collective-permute-start.31 = (bf16[176,256]{1,0:T(8,128)(2,1)S(1)}, bf16[176,256]{1,0:T(8,128)(2,1)S(1)}, u32[]{:S(2)}, u32[]{:S(2)}) collective-permute-start(bf16[176,256]{1,0:T(8,128)(2,1)S(1)} %add_convert_fusion.4), channel_id=1, source_target_pairs={{0,7},{1,0},{2,1},{3,2},{4,3},{5,4},{6,5},{7,6},{8,15},{9,8},{10,9... | collective-permute-start | bytes 270344 | tf_op jit(solution)/shard_map/ppermute | solution.py:122
  134.2 4.3 %collective-permute-start.33 = (bf16[176,256]{1,0:T(8,128)(2,1)S(1)}, bf16[176,256]{1,0:T(8,128)(2,1)S(1)}, u32[]{:S(2)}, u32[]{:S(2)}) collective-permute-start(bf16[176,256]{1,0:T(8,128)(2,1)S(1)} %get-tuple-element.126.refs_5_), channel_id=1, source_target_pairs={{0,6},{1,7},{2,0},{3,1},{4,2},{5,3},{6,4},{7,5},{8,14},{9,15},{10,... | collective-permute-start | bytes 270344 | tf_op jit(solution)/shard_map/ppermute | solution.py:122
  135.4 6.1 %collective-permute-start.32 = (bf16[176,256]{1,0:T(8,128)(2,1)S(1)}, bf16[176,256]{1,0:T(8,128)(2,1)S(1)}, u32[]{:S(2)}, u32[]{:S(2)}) collective-permute-start(bf16[176,256]{1,0:T(8,128)(2,1)S(1)} %get-tuple-element.126.refs_5_), channel_id=1, source_target_pairs={{0,7},{1,0},{2,1},{3,2},{4,3},{5,4},{6,5},{7,6},{8,15},{9,8},{10,9... | collective-permute-start | bytes 270344 | tf_op jit(solution)/shard_map/ppermute | solution.py:122
  136.4 6.8 %collective-permute-start.35 = (bf16[176,256]{1,0:T(8,128)(2,1)S(1)}, bf16[176,256]{1,0:T(8,128)(2,1)S(1)}, u32[]{:S(2)}, u32[]{:S(2)}) collective-permute-start(bf16[176,256]{1,0:T(8,128)(2,1)S(1)} %get-tuple-element.126.refs_5_), channel_id=1, source_target_pairs={{0,1},{1,2},{2,3},{3,4},{4,5},{5,6},{6,7},{7,0},{8,9},{9,10},{10,1... | collective-permute-start | bytes 270344 | tf_op jit(solution)/shard_map/ppermute | solution.py:122
  137.4 5.8 %collective-permute-start.34 = (bf16[176,256]{1,0:T(8,128)(2,1)S(1)}, bf16[176,256]{1,0:T(8,128)(2,1)S(1)}, u32[]{:S(2)}, u32[]{:S(2)}) collective-permute-start(bf16[176,256]{1,0:T(8,128)(2,1)S(1)} %get-tuple-element.126.refs_5_), channel_id=1, source_target_pairs={{0,2},{1,3},{2,4},{3,5},{4,6},{5,7},{6,0},{7,1},{8,10},{9,11},{10,... | collective-permute-start | bytes 270344 | tf_op jit(solution)/shard_map/ppermute | solution.py:122
  141.5 7.6 %collective-permute-start.36 = (bf16[176,384]{1,0:T(8,128)(2,1)S(1)}, bf16[176,384]{1,0:T(8,128)(2,1)S(1)}, u32[]{:S(2)}, u32[]{:S(2)}) collective-permute-start(bf16[176,384]{1,0:T(8,128)(2,1)S(1)} %pad_maximum_fusion), channel_id=1, source_target_pairs={{0,6},{1,7},{2,0},{3,1},{4,2},{5,3},{6,4},{7,5},{8,14},{9,15},{10,... | collective-permute-start | bytes 405512 | tf_op jit(solution)/shard_map/ppermute | solution.py:122
  143.2 6.4 %collective-permute-start.37 = (bf16[176,384]{1,0:T(8,128)(2,1)S(1)}, bf16[176,384]{1,0:T(8,128)(2,1)S(1)}, u32[]{:S(2)}, u32[]{:S(2)}) collective-permute-start(bf16[176,384]{1,0:T(8,128)(2,1)S(1)} %pad_maximum_fusion.1), channel_id=1, source_target_pairs={{0,2},{1,3},{2,4},{3,5},{4,6},{5,7},{6,0},{7,1},{8,10},{9,11},{10,... | collective-permute-start | bytes 405512 | tf_op jit(solution)/shard_map/ppermute | solution.py:122

commit v2 on v1

--- a/solution.py
+++ b/solution.py
@@ -102,7 +102,7 @@
     early = [line, plus, minus]
     swapped = [send(v, swap_core()) for v in early]
     two, done = lax.optimization_barrier((two, beside(early)))
-    return early, [two] + swapped + [send(two, swap_core())], done
+    return early, swapped, [two, send(two, swap_core())], done
 
 
 def source_slots(col_ids):
@@ -113,8 +113,9 @@
     other = device & 1
     along_first = jnp.where(other == 0, dy, dx)
     along_second = jnp.where(other == 0, dx, dy)
-    line = jnp.where(along_second > 1, 5 - along_second, along_second)
-    line = ((other ^ me) & 1) * 4 + line
+    swapped = (other ^ me) & 1
+    line = swapped * 3 + jnp.where(along_second == 3, 2, along_second)
+    line = jnp.where(along_second == 2, 6 + swapped, line)
     return (line * 4 + along_first) * 2 + (col_ids & 1)
 
 
@@ -340,16 +341,19 @@
 
 
 def logits_early_kernel(*refs):
-    table, (tiles, weight_one_t, weight_two_t, begun, *rest) = refs[:4], refs[4:]
+    table, (tiles, weight_one_t, weight_two_t, *rest) = refs[:4], refs[4:]
+    begun, rest = rest[:2], rest[2:]
     pieces, rest = rest[:-7], rest[-7:]
     source, out_up, out_down, agg, hidden_t, slope_t, total = rest
-    blocks = begun.shape[0]
-
-    def step(i, carry):
-        source[i] = begun[i]
-        return carry
-
-    lax.fori_loop(0, blocks, step, 0)
+    blocks = 0
+    for part in begun:
+
+        def step(i, carry):
+            source[blocks + i] = part[i]
+            return carry
+
+        lax.fori_loop(0, part.shape[0], step, 0)
+        blocks += part.shape[0]
     later = source.at[pl.ds(blocks, 64 - blocks)]
     gates(pieces, weight_one_t, weight_two_t, later, agg, hidden_t, slope_t)
     source[64] = jnp.zeros((CPAD, TB), BF16)
@@ -492,7 +496,7 @@
 
 def backward_late_kernel(*refs):
     table, (tiles, weight_two, begun, *rest) = refs[:4], refs[4:]
-    panels, (up, down, *rest) = (rest[0:3], rest[3:6]), rest[6:]
+    panels, (up, down, *rest) = (rest[0:3], rest[3:6], rest[6:9]), rest[9:]
     out, grads, total, sum_one, sum_two = rest
     for place, piece in enumerate((up, down)):
         for k in range(3):
@@ -598,28 +602,29 @@
         *ready, tiles = lax.optimization_barrier(ready)
         return (*ready, hold_tiles(tiles, early[0]))
 
-    early, late, done = gather_row(features, prepare)
+    *pieces, done = gather_row(features, prepare)
     forward, reverse, labels, place, tiles = done
     parts, _ = spread_and_reduce(
         aggregate_early_kernel,
         aggregate_late_kernel,
         "aggregate",
         forward,
-        (tiles, *early, *late),
+        (tiles, *pieces[0], *pieces[1], *pieces[2]),
         (),
         (TB, FEAT),
         (ROWS, FEAT),
     )
     agg, weight_one_t, weight_two_t, weight_two = middle(parts, weight_one, second_t)
-    early, late, begun = gather_row(
+    _, swapped, late, begun = gather_row(
         agg, functools.partial(early_gates, weight_one_t, weight_two_t)
     )
+    more = early_gates(weight_one_t, weight_two_t, swapped)
     parts, panel = spread_and_reduce(
         logits_early_kernel,
         logits_late_kernel,
         "partial_logits",
         forward,
-        (tiles, weight_one_t, weight_two_t, begun[0], *late),
+        (tiles, weight_one_t, weight_two_t, begun[0], more[0], *late),
         panel_shapes(sum(p.shape[0] for p in late)),
         (CPAD, TB),
         (CPAD, ROWS),
@@ -628,7 +633,7 @@
     near, up, down = gather_col(grad_t)
     total = backward_early(reverse, tiles, near)
     grads = backward_late(
-        reverse, tiles, weight_two, total, (*begun[1:], *panel), up, down
+        reverse, tiles, weight_two, total, (*begun[1:], *more[1:], *panel), up, down
     )
     grad_one, grad_two_t = unpack(sum_everywhere(grads))
     return logits_t.T, grad_one, grad_two_t.T

time: 204 us -> 202 us (level)
  starting transfers between devices: 56.3 us -> 63.2 us
  blocking collectives: 44.6 us -> 39.4 us
  waiting for transfers between devices: 59.3 us -> 56 us
    ppermute x18, starting transfers between devices: 27.1 us -> 32.4 us  [along_col(): return lax.ppermute(value, 'col', [(i, (i + step) % GZ) for i in range(GZ)])]
    all_to_all x1, blocking collectives: 19.1 us -> 14.1 us  [sum_everywhere(): lax.all_to_all(grads.reshape(32, 16, FEAT), 'row', 0, 0, tiled=True)]
    ppermute x18, waiting for transfers between devices: 29 us -> 24.5 us  [along_col(): return lax.ppermute(value, 'col', [(i, (i + step) % GZ) for i in range(GZ)])]
    pallas_call x2, Pallas kernels: 8.73 us -> 5.71 us  [spread_and_reduce(): pl.pallas_call(early_kernel, name=name + '_early', out_shape=(jax.ShapeDt...]
    pallas_call x1 -> x2, Pallas kernels: 2.45 us -> 4.9 us  [early_gates(): pl.pallas_call(gates_kernel, name='early_gates', out_shape=(jax.ShapeDtyp...]
  transfers between devices with their start and end apart: 38 -> 38, of which waited for: 24 -> 22; matrix products, arithmetic and copies ran while one was open for 3% -> 3% of each run, Pallas kernels for 6% -> 7%
where the time goes in v2:
time: 202 us; the launch traced here: 200 us
  starting transfers between devices  63.2 us (31%)
  waiting for transfers between devices  56 us (28%)
  blocking collectives  39.4 us (20%)
  Pallas kernels  29.6 us (15%)
  other arithmetic  4.42 us (2%)
  between operations  4.1 us (2%)
  local copies, waits for them, and re-layouts  3.27 us (2%)
    ppermute x18, starting transfers between devices, along_col(): return lax.ppermute(value, 'col', [(i, (i + step) % GZ) for i in range(GZ)])  32.4 us
    ppermute x20, waiting for transfers between devices, gather_row(): send = lambda v, perm: lax.ppermute(v, 'row', perm)  31.4 us
    ppermute x20, starting transfers between devices, gather_row(): send = lambda v, perm: lax.ppermute(v, 'row', perm)  30.7 us
    ppermute x18, waiting for transfers between devices, along_col(): return lax.ppermute(value, 'col', [(i, (i + step) % GZ) for i in range(GZ)])  24.5 us
    all_to_all x1, blocking collectives, sum_everywhere(): lax.all_to_all(grads.reshape(32, 16, FEAT), 'row', 0, 0, tiled=True)  14.1 us
    all_to_all x1, blocking collectives, sum_everywhere(): lax.all_to_all(jnp.broadcast_to(share, (32, 16, FEAT)), 'row', 0, 0, tile...  13.9 us
    all_to_all x1, blocking collectives, sum_everywhere(): lax.all_to_all(jnp.broadcast_to(share, (GZ, 16, FEAT)), 'col', 0, 0, tile...  11.4 us
    pallas_call x1, Pallas kernels, backward_late(): pl.pallas_call(backward_late_kernel, name='backward_late', out_shape=jax....  8.32 us
  transfers between devices with their start and end apart: 38, of which 22 were waited for; matrix products, arithmetic and copies ran while one was open for 3% of the time, Pallas kernels for 7%

profile of v2, /device:TPU:1, one launch (start us, length us, event | category | flops | bytes accessed | tf_op | source)
XLA Modules:
  0.0 200.0 jit_solution(5719485078635439073)
XLA Ops:
  0.6 3.4 %collective-permute-start = (bf16[256,256]{1,0:T(8,128)(2,1)}, bf16[256,256]{1,0:T(8,128)(2,1)S(1)}, u32[]{:S(2)}, u32[]{:S(2)}) collective-permute-start(bf16[256,256]{1,0:T(8,128)(2,1)} %param.8), channel_id=1, source_target_pairs={{0,48},{8,200},{16,0},{24,216},{32,16},{40,232},{48,32},{56,248},{... | collective-permute-start | bytes 393224 | tf_op jit(solution)/shard_map/ppermute | solution.py:88
  5.1 0.9 constant_dynamic-update-slice_fusion.3
  6.1 1.6 collective-permute-done
  7.7 2.0 collective-permute-done.1
  9.7 1.6 collective-permute-done.2
  11.3 2.5 %collective-permute-start.4 = (bf16[1024,256]{1,0:T(8,128)(2,1)S(1)}, bf16[1024,256]{1,0:T(8,128)(2,1)S(1)}, u32[]{:S(2)}, u32[]{:S(2)}) collective-permute-start(bf16[1024,256]{1,0:T(8,128)(2,1)S(1)} %constant_dynamic-update-slice_fusion.after.refs_5_), channel_id=1, source_target_pairs={{0,192},{8,56},{16,208},{24,8},{32,224},{40,24},{48,240},{56,40},{... | collective-permute-start | bytes 1572872 | tf_op jit(solution)/shard_map/ppermute | solution.py:88
  15.6 9.9 %collective-permute-done.4.refs_6_ = bf16[1024,256]{1,0:T(8,128)(2,1)S(1)} collective-permute-done((bf16[1024,256]{1,0:T(8,128)(2,1)S(1)}, bf16[1024,256]{1,0:T(8,128)(2,1)S(1)}, u32[]{:S(2)}, u32[]{:S(2)}) %collective-permute-start.4) | collective-permute-done | bytes 524320 | tf_op jit(solution)/shard_map/ppermute | solution.py:88
  27.2 3.0 %collective-permute-start.6 = (bf16[1024,256]{1,0:T(8,128)(2,1)S(1)}, bf16[1024,256]{1,0:T(8,128)(2,1)S(1)}, u32[]{:S(2)}, u32[]{:S(2)}) collective-permute-start(bf16[1024,256]{1,0:T(8,128)(2,1)S(1)} %constant_dynamic-update-slice_fusion.after.refs_5_), channel_id=1, source_target_pairs={{0,8},{8,0},{16,24},{24,16},{32,40},{40,32},{48,56},{56,48},{64,72... | collective-permute-start | bytes 1572872 | tf_op jit(solution)/shard_map/ppermute | solution.py:88
  35.2 2.2 %copy-done = bf16[1,1,128,128,128]{4,3,2,1,0:T(8,128)(2,1)S(1)} copy-done((bf16[1,1,128,128,128]{4,3,2,1,0:T(8,128)(2,1)S(1)}, bf16[1,1,128,128,128]{4,3,2,1,0:T(8,128)(2,1)}, u32[]{:S(2)}) %copy-start) | copy-done | bytes 4194328
  38.4 1.3 collective-permute-done.7.refs_9_
  41.2 2.1 %aggregate_early.1 = (bf16[65,128,256]{2,1,0:T(8,128)(2,1)S(1)}, bf16[256,384]{1,0:T(8,128)(2,1)S(1)}, bf16[256,384]{1,0:T(8,128)(2,1)S(1)}) custom-call(s32[208]{0:T(256)S(1)} %get-tuple-element.88.refs_0_, s32[208]{0:T(256)S(1)} %broadcast_add_fusion.1.refs_1_, s32[52]{0:T(128)S(1)} %select_reduce_fusion.6.refs_2_, s32[2]{0:T(128)S(1)} %get-tuple-element.91.refs_3_, ...), custom_call_target="tpu_custom_call" | custom-call | flops 1000000000 | bytes 10000000 | tf_op jit(solution)/shard_map/aggregate_early/pallas_call | solution.py:377
  43.3 3.4 %collective-permute-start.10 = (bf16[256,384]{1,0:T(8,128)(2,1)S(1)}, bf16[256,384]{1,0:T(8,128)(2,1)S(1)}, u32[]{:S(2)}, u32[]{:S(2)}) collective-permute-start(bf16[256,384]{1,0:T(8,128)(2,1)S(1)} %get-tuple-element.98), channel_id=1, source_target_pairs={{0,2},{1,3},{2,4},{3,5},{4,6},{5,7},{6,0},{7,1},{8,10},{9,11},{10,... | collective-permute-start | bytes 589832 | tf_op jit(solution)/shard_map/ppermute | solution.py:123
  46.6 2.5 %collective-permute-start.12 = (bf16[256,384]{1,0:T(8,128)(2,1)S(1)}, bf16[256,384]{1,0:T(8,128)(2,1)S(1)}, u32[]{:S(2)}, u32[]{:S(2)}) collective-permute-start(bf16[256,384]{1,0:T(8,128)(2,1)S(1)} %get-tuple-element.100), channel_id=1, source_target_pairs={{0,6},{1,7},{2,0},{3,1},{4,2},{5,3},{6,4},{7,5},{8,14},{9,15},{10,... | collective-permute-start | bytes 589832 | tf_op jit(solution)/shard_map/ppermute | solution.py:123
  49.1 2.4 %aggregate_late.1 = (f32[256,256]{1,0:T(8,128)S(1)}, f32[256,256]{1,0:T(8,128)S(1)}, f32[256,256]{1,0:T(8,128)S(1)}, f32[256,256]{1,0:T(8,128)S(1)}, f32[256,256]{1,0:T(8,128)S(1)}) custom-call(s32[208]{0:T(256)S(1)} %get-tuple-element.88.refs_0_, s32[208]{0:T(256)S(1)} %broadcast_add_fusion.1.refs_1_, s32[52]{0:T(128)S(1)} %select_reduce_fusion.6.refs_2_, ...), custom_call_target="tpu_custom_call" | custom-call | flops 1000000000 | bytes 10000000 | tf_op jit(solution)/shard_map/aggregate_late/pallas_call | solution.py:387
  51.6 4.5 %collective-permute-done.10 = bf16[256,384]{1,0:T(8,128)(2,1)S(1)} collective-permute-done((bf16[256,384]{1,0:T(8,128)(2,1)S(1)}, bf16[256,384]{1,0:T(8,128)(2,1)S(1)}, u32[]{:S(2)}, u32[]{:S(2)}) %collective-permute-start.10) | collective-permute-done | bytes 196640 | tf_op jit(solution)/shard_map/ppermute | solution.py:123
  56.1 3.3 %collective-permute-start.11 = (bf16[256,256]{1,0:T(8,128)(2,1)S(1)}, bf16[256,256]{1,0:T(8,128)(2,1)S(1)}, u32[]{:S(2)}, u32[]{:S(2)}) collective-permute-start(bf16[256,256]{1,0:T(8,128)(2,1)S(1)} %add_convert_fusion.3), channel_id=1, source_target_pairs={{0,2},{1,3},{2,4},{3,5},{4,6},{5,7},{6,0},{7,1},{8,10},{9,11},{10,... | collective-permute-start | bytes 393224 | tf_op jit(solution)/shard_map/ppermute | solution.py:123
  60.0 2.0 collective-permute-start.13
  62.9 2.2 %collective-permute-start.15 = (bf16[256,256]{1,0:T(8,128)(2,1)S(1)}, bf16[256,256]{1,0:T(8,128)(2,1)S(1)}, u32[]{:S(2)}, u32[]{:S(2)}) collective-permute-start(bf16[256,256]{1,0:T(8,128)(2,1)S(1)} %add_convert_fusion), channel_id=1, source_target_pairs={{0,7},{1,0},{2,1},{3,2},{4,3},{5,4},{6,5},{7,6},{8,15},{9,8},{10,9... | collective-permute-start | bytes 393224 | tf_op jit(solution)/shard_map/ppermute | solution.py:123
  65.0 3.7 %collective-permute-done.13.refs_2_ = bf16[256,256]{1,0:T(8,128)(2,1)S(1)} collective-permute-done((bf16[256,256]{1,0:T(8,128)(2,1)S(1)}, bf16[256,256]{1,0:T(8,128)(2,1)S(1)}, u32[]{:S(2)}, u32[]{:S(2)}) %collective-permute-start.13) | collective-permute-done | bytes 131104 | tf_op jit(solution)/shard_map/ppermute | solution.py:123
  68.8 2.5 %collective-permute-done.15.refs_4_ = bf16[256,256]{1,0:T(8,128)(2,1)S(1)} collective-permute-done((bf16[256,256]{1,0:T(8,128)(2,1)S(1)}, bf16[256,256]{1,0:T(8,128)(2,1)S(1)}, u32[]{:S(2)}, u32[]{:S(2)}) %collective-permute-start.15) | collective-permute-done | bytes 131104 | tf_op jit(solution)/shard_map/ppermute | solution.py:123
  71.5 4.3 %collective-permute-start.16 = (bf16[256,256]{1,0:T(8,128)(2,1)S(1)}, bf16[256,256]{1,0:T(8,128)(2,1)S(1)}, u32[]{:S(2)}, u32[]{:S(2)}) collective-permute-start(bf16[256,256]{1,0:T(8,128)(2,1)S(1)} %get-tuple-element.105), channel_id=1, source_target_pairs={{0,48},{8,200},{16,0},{24,216},{32,16},{40,232},{48,32},{56,248},{... | collective-permute-start | bytes 393224 | tf_op jit(solution)/shard_map/ppermute | solution.py:88
  76.5 2.5 %collective-permute-done.16 = bf16[256,256]{1,0:T(8,128)(2,1)S(1)} collective-permute-done((bf16[256,256]{1,0:T(8,128)(2,1)S(1)}, bf16[256,256]{1,0:T(8,128)(2,1)S(1)}, u32[]{:S(2)}, u32[]{:S(2)}) %collective-permute-start.16) | collective-permute-done | bytes 131104 | tf_op jit(solution)/shard_map/ppermute | solution.py:88
  79.1 2.1 %collective-permute-done.17 = bf16[256,256]{1,0:T(8,128)(2,1)S(1)} collective-permute-done((bf16[256,256]{1,0:T(8,128)(2,1)S(1)}, bf16[256,256]{1,0:T(8,128)(2,1)S(1)}, u32[]{:S(2)}, u32[]{:S(2)}) %collective-permute-start.17) | collective-permute-done | bytes 131104 | tf_op jit(solution)/shard_map/ppermute | solution.py:88
  81.2 1.1 collective-permute-done.18
  84.3 6.4 %collective-permute-done.20.rest_1_ = bf16[1024,256]{1,0:T(8,128)(2,1)S(1)} collective-permute-done((bf16[1024,256]{1,0:T(8,128)(2,1)S(1)}, bf16[1024,256]{1,0:T(8,128)(2,1)S(1)}, u32[]{:S(2)}, u32[]{:S(2)}) %collective-permute-start.20) | collective-permute-done | bytes 524320 | tf_op jit(solution)/shard_map/ppermute | solution.py:88
  90.7 8.0 %collective-permute-start.22 = (bf16[1024,256]{1,0:T(8,128)(2,1)S(1)}, bf16[1024,256]{1,0:T(8,128)(2,1)S(1)}, u32[]{:S(2)}, u32[]{:S(2)}) collective-permute-start(bf16[1024,256]{1,0:T(8,128)(2,1)S(1)} %constant_dynamic-update-slice_fusion.4.rest_0_), channel_id=1, source_target_pairs={{0,8},{8,0},{16,24},{24,16},{32,40},{40,32},{48,56},{56,48},{64,72... | collective-permute-start | bytes 1572872 | tf_op jit(solution)/shard_map/ppermute | solution.py:88
  98.7 2.4 %early_gates.2 = (bf16[24,176,128]{2,1,0:T(8,128)(2,1)S(1)}, bf16[3072,256]{1,0:T(8,128)(2,1)S(1)}, bf16[256,3072]{1,0:T(8,128)(2,1)S(1)}, bf16[256,3072]{1,0:T(8,128)(2,1)S(1)}) custom-call(bf16[256,256]{1,0:T(8,128)(2,1)S(1)} %get-tuple-element.103.weight_one_t.refs_5_, bf16[176,256]{1,0:T(8,128)(2,1)S(1)} %get-tuple-element.104.weight_two_t.refs_6_, ...), custom_call_target="tpu_custom_call" | custom-call | flops 1000 | bytes 1000 | tf_op jit(solution)/shard_map/early_gates/pallas_call | solution.py:329
  101.2 3.8 %collective-permute-start.24 = (bf16[1024,256]{1,0:T(8,128)(2,1)S(1)}, bf16[1024,256]{1,0:T(8,128)(2,1)S(1)}, u32[]{:S(2)}, u32[]{:S(2)}) collective-permute-start(bf16[1024,256]{1,0:T(8,128)(2,1)S(1)} %collective-permute-done.21.rest_2_), channel_id=1, source_target_pairs={{0,8},{8,0},{16,24},{24,16},{32,40},{40,32},{48,56},{56,48},{64,72... | collective-permute-start | bytes 1572872 | tf_op jit(solution)/shard_map/ppermute | solution.py:88
  105.1 1.4 collective-permute-done.24.rest_2_
  106.5 2.4 %early_gates.3 = (bf16[24,176,128]{2,1,0:T(8,128)(2,1)S(1)}, bf16[3072,256]{1,0:T(8,128)(2,1)S(1)}, bf16[256,3072]{1,0:T(8,128)(2,1)S(1)}, bf16[256,3072]{1,0:T(8,128)(2,1)S(1)}) custom-call(bf16[256,256]{1,0:T(8,128)(2,1)S(1)} %get-tuple-element.103.weight_one_t.refs_5_, bf16[176,256]{1,0:T(8,128)(2,1)S(1)} %get-tuple-element.104.weight_two_t.refs_6_, ...), custom_call_target="tpu_custom_call" | custom-call | flops 1000 | bytes 1000 | tf_op jit(solution)/shard_map/early_gates/pallas_call | solution.py:329
  109.0 3.6 %partial_logits_early.1 = (bf16[65,176,128]{2,1,0:T(8,128)(2,1)S(1)}, bf16[176,384]{1,0:T(8,128)(2,1)S(1)}, bf16[176,384]{1,0:T(8,128)(2,1)S(1)}, bf16[2048,256]...) custom-call(s32[208]{0:T(256)S(1)} %get-tuple-element.88.refs_0_, ...), custom_call_target="tpu_custom_call" | custom-call | flops 1000000000 | bytes 10000000 | tf_op jit(solution)/shard_map/partial_logits_early/pallas_call | solution.py:377
  112.6 1.5 collective-permute-start.26
  114.1 2.1 %collective-permute-start.28 = (bf16[176,384]{1,0:T(8,128)(2,1)S(1)}, bf16[176,384]{1,0:T(8,128)(2,1)S(1)}, u32[]{:S(2)}, u32[]{:S(2)}) collective-permute-start(bf16[176,384]{1,0:T(8,128)(2,1)S(1)} %get-tuple-element.120), channel_id=1, source_target_pairs={{0,6},{1,7},{2,0},{3,1},{4,2},{5,3},{6,4},{7,5},{8,14},{9,15},{10,... | collective-permute-start | bytes 405512 | tf_op jit(solution)/shard_map/ppermute | solution.py:123
  116.3 2.5 %partial_logits_late.1 = (f32[176,256]{1,0:T(8,128)S(1)}, f32[176,256]{1,0:T(8,128)S(1)}, f32[176,256]{1,0:T(8,128)S(1)}, f32[176,256]{1,0:T(8,128)S(1)}, f32[176,256]{1,0:T(8,128)S(1)}) custom-call(s32[208]{0:T(256)S(1)} %get-tuple-element.88.refs_0_, s32[208]{0:T(256)S(1)} %broadcast_add_fusion.1.refs_1_, s32[52]{0:T(128)S(1)} %select_reduce_fusion.6.refs_2_, ...), custom_call_target="tpu_custom_call" | custom-call | flops 1000000000 | bytes 10000000 | tf_op jit(solution)/shard_map/partial_logits_late/pallas_call | solution.py:387
  118.8 4.2 %collective-permute-done.26 = bf16[176,384]{1,0:T(8,128)(2,1)S(1)} collective-permute-done((bf16[176,384]{1,0:T(8,128)(2,1)S(1)}, bf16[176,384]{1,0:T(8,128)(2,1)S(1)}, u32[]{:S(2)}, u32[]{:S(2)}) %collective-permute-start.26) | collective-permute-done | bytes 135200 | tf_op jit(solution)/shard_map/ppermute | solution.py:123
  123.5 3.4 %collective-permute-start.29 = (bf16[176,256]{1,0:T(8,128)(2,1)S(1)}, bf16[176,256]{1,0:T(8,128)(2,1)S(1)}, u32[]{:S(2)}, u32[]{:S(2)}) collective-permute-start(bf16[176,256]{1,0:T(8,128)(2,1)S(1)} %add_convert_fusion.6), channel_id=1, source_target_pairs={{0,6},{1,7},{2,0},{3,1},{4,2},{5,3},{6,4},{7,5},{8,14},{9,15},{10,... | collective-permute-start | bytes 270344 | tf_op jit(solution)/shard_map/ppermute | solution.py:123
  127.1 2.7 %collective-permute-start.31 = (bf16[176,256]{1,0:T(8,128)(2,1)S(1)}, bf16[176,256]{1,0:T(8,128)(2,1)S(1)}, u32[]{:S(2)}, u32[]{:S(2)}) collective-permute-start(bf16[176,256]{1,0:T(8,128)(2,1)S(1)} %add_convert_fusion.4), channel_id=1, source_target_pairs={{0,7},{1,0},{2,1},{3,2},{4,3},{5,4},{6,5},{7,6},{8,15},{9,8},{10,9... | collective-permute-start | bytes 270344 | tf_op jit(solution)/shard_map/ppermute | solution.py:123
  129.8 1.9 collective-permute-done.30.refs_3_
  132.4 3.2 %collective-permute-start.33 = (bf16[176,256]{1,0:T(8,128)(2,1)S(1)}, bf16[176,256]{1,0:T(8,128)(2,1)S(1)}, u32[]{:S(2)}, u32[]{:S(2)}) collective-permute-start(bf16[176,256]{1,0:T(8,128)(2,1)S(1)} %get-tuple-element.131.refs_5_), channel_id=1, source_target_pairs={{0,6},{1,7},{2,0},{3,1},{4,2},{5,3},{6,4},{7,5},{8,14},{9,15},{10,... | collective-permute-start | bytes 270344 | tf_op jit(solution)/shard_map/ppermute | solution.py:123
  135.6 1.9 collective-permute-start.34
  137.6 2.4 %collective-permute-done.32.refs_6_ = bf16[176,256]{1,0:T(8,128)(2,1)S(1)} collective-permute-done((bf16[176,256]{1,0:T(8,128)(2,1)S(1)}, bf16[176,256]{1,0:T(8,128)(2,1)S(1)}, u32[]{:S(2)}, u32[]{:S(2)}) %collective-permute-start.32) | collective-permute-done | bytes 90144 | tf_op jit(solution)/shard_map/ppermute | solution.py:123
  140.1 2.5 %collective-permute-start.36 = (bf16[176,384]{1,0:T(8,128)(2,1)S(1)}, bf16[176,384]{1,0:T(8,128)(2,1)S(1)}, u32[]{:S(2)}, u32[]{:S(2)}) collective-permute-start(bf16[176,384]{1,0:T(8,128)(2,1)S(1)} %pad_maximum_fusion), channel_id=1, source_target_pairs={{0,6},{1,7},{2,0},{3,1},{4,2},{5,3},{6,4},{7,5},{8,14},{9,15},{10,... | collective-permute-start | bytes 405512 | tf_op jit(solution)/shard_map/ppermute | solution.py:123
  143.4 3.8 %backward_early.1.refs_6_ = f32[64,176,128]{2,1,0:T(8,128)S(1)} custom-call(s32[272]{0:T(512)S(1)} %get-tuple-element.126.refs_0_, s32[272]{0:T(512)S(1)} %broadcast_add_fusion.refs_1_, s32[136]{0:T(256)S(1)} %select_reduce_fusion.4.refs_2_, s32[2]{0:T(128)S(1)} %get-tuple-element.129.refs_3_, bf16[128,128,128]{2,1,0:T(8,128)(2,1)S(1)} %hold_tiles.1.refs_4_, ...), custom_call_target="tpu_custom_call" | custom-call | flops 1000 | bytes 1000 | tf_op jit(solution)/shard_map/backward_early/pallas_call | solution.py:485
  147.2 4.1 %collective-permute-done.37.refs_17_ = bf16[176,384]{1,0:T(8,128)(2,1)S(1)} collective-permute-done((bf16[176,384]{1,0:T(8,128)(2,1)S(1)}, bf16[176,384]{1,0:T(8,128)(2,1)S(1)}, u32[]{:S(2)}, u32[]{:S(2)}) %collective-permute-start.37) | collective-permute-done | bytes 135200 | tf_op jit(solution)/shard_map/ppermute | solution.py:123
  151.3 8.3 %backward_late.1 = bf16[512,256]{1,0:T(8,128)(2,1)S(1)} custom-call(s32[272]{0:T(512)S(1)} %get-tuple-element.126.refs_0_, s32[272]{0:T(512)S(1)} %broadcast_add_fusion.refs_1_, s32[136]{0:T(256)S(1)} %select_reduce_fusion.4.refs_2_, s32[2]{0:T(128)S(1)} %get-tuple-element.129.refs_3_, bf16[128,128,128]{2,1,0:T(8,128)(2,1)S(1)} %hold_tiles.1.refs_4_, ...), custom_call_target="tpu_custom_call" | custom-call | flops 5000000000 | bytes 20000000 | tf_op jit(solution)/shard_map/backward_late/pallas_call | solution.py:537
  159.7 14.1 %all_to_all.15 = bf16[32,16,256]{2,1,0:T(8,128)(2,1)S(1)} all-to-all(bf16[32,16,256]{2,1,0:T(8,128)(2,1)S(1)} %bitcast.14), channel_id=1, replica_groups=mesh['row'=32,'col'=8] {'row'}, dimensions={0} | all-to-all | bytes 524288 | tf_op jit(solution)/shard_map/all_to_all | solution.py:555
  173.9 11.4 %all_to_all.16 = bf16[8,16,256]{2,1,0:T(8,128)(2,1)S(1)} all-to-all(bf16[8,16,256]{2,1,0:T(8,128)(2,1)S(1)} %broadcast_in_dim.224), channel_id=1, replica_groups=mesh['row'=32,'col'=8] {'col'}, dimensions={0} | all-to-all | bytes 131072 | tf_op jit(solution)/shard_map/all_to_all | solution.py:557
  185.3 13.9 %all_to_all.17 = bf16[32,16,256]{2,1,0:T(8,128)(2,1)S(1)} all-to-all(bf16[32,16,256]{2,1,0:T(8,128)(2,1)S(1)} %broadcast_in_dim.225), channel_id=1, replica_groups=mesh['row'=32,'col'=8] {'row'}, dimensions={0} | all-to-all | bytes 524288 | tf_op jit(solution)/shard_map/all_to_all | solution.py:561
  (101 shorter events, 17.0 us)
Async XLA Ops:
  0.6 7.1 %collective-permute-start = (bf16[256,256]{1,0:T(8,128)(2,1)}, bf16[256,256]{1,0:T(8,128)(2,1)S(1)}, u32[]{:S(2)}, u32[]{:S(2)}) collective-permute-start(bf16[256,256]{1,0:T(8,128)(2,1)} %param.8), channel_id=1, source_target_pairs={{0,48},{8,200},{16,0},{24,216},{32,16},{40,232},{48,32},{56,248},{... | collective-permute-start | bytes 393224 | tf_op jit(solution)/shard_map/ppermute | solution.py:88
  4.0 5.6 %collective-permute-start.1 = (bf16[256,256]{1,0:T(8,128)(2,1)}, bf16[256,256]{1,0:T(8,128)(2,1)S(1)}, u32[]{:S(2)}, u32[]{:S(2)}) collective-permute-start(bf16[256,256]{1,0:T(8,128)(2,1)} %param.8), channel_id=1, source_target_pairs={{0,32},{8,136},{16,48},{24,152},{32,0},{40,168},{48,16},{56,184},{... | collective-permute-start | bytes 393224 | tf_op jit(solution)/shard_map/ppermute | solution.py:88
  4.5 6.7 %collective-permute-start.2 = (bf16[256,256]{1,0:T(8,128)(2,1)}, bf16[256,256]{1,0:T(8,128)(2,1)S(1)}, u32[]{:S(2)}, u32[]{:S(2)}) collective-permute-start(bf16[256,256]{1,0:T(8,128)(2,1)} %param.8), channel_id=1, source_target_pairs={{0,16},{8,72},{16,32},{24,88},{32,48},{40,104},{48,0},{56,120},{64... | collective-permute-start | bytes 393224 | tf_op jit(solution)/shard_map/ppermute | solution.py:88
  11.3 14.3 %collective-permute-start.4 = (bf16[1024,256]{1,0:T(8,128)(2,1)S(1)}, bf16[1024,256]{1,0:T(8,128)(2,1)S(1)}, u32[]{:S(2)}, u32[]{:S(2)}) collective-permute-start(bf16[1024,256]{1,0:T(8,128)(2,1)S(1)} %constant_dynamic-update-slice_fusion.after.refs_5_), channel_id=1, source_target_pairs={{0,192},{8,56},{16,208},{24,8},{32,224},{40,24},{48,240},{56,40},{... | collective-permute-start | bytes 1572872 | tf_op jit(solution)/shard_map/ppermute | solution.py:88
  14.5 23.2 %collective-permute-start.3 = (bf16[1024,256]{1,0:T(8,128)(2,1)S(1)}, bf16[1024,256]{1,0:T(8,128)(2,1)S(1)}, u32[]{:S(2)}, u32[]{:S(2)}) collective-permute-start(bf16[1024,256]{1,0:T(8,128)(2,1)S(1)} %constant_dynamic-update-slice_fusion.after.refs_5_), channel_id=1, source_target_pairs={{0,128},{8,40},{16,144},{24,56},{32,160},{40,8},{48,176},{56,24},{... | collective-permute-start | bytes 1572872 | tf_op jit(solution)/shard_map/ppermute | solution.py:88
  14.9 22.9 %collective-permute-start.5 = (bf16[1024,256]{1,0:T(8,128)(2,1)S(1)}, bf16[1024,256]{1,0:T(8,128)(2,1)S(1)}, u32[]{:S(2)}, u32[]{:S(2)}) collective-permute-start(bf16[1024,256]{1,0:T(8,128)(2,1)S(1)} %constant_dynamic-update-slice_fusion.after.refs_5_), channel_id=1, source_target_pairs={{0,64},{8,24},{16,80},{24,40},{32,96},{40,56},{48,112},{56,8},{64,... | collective-permute-start | bytes 1572872 | tf_op jit(solution)/shard_map/ppermute | solution.py:88
  27.2 11.2 %collective-permute-start.6 = (bf16[1024,256]{1,0:T(8,128)(2,1)S(1)}, bf16[1024,256]{1,0:T(8,128)(2,1)S(1)}, u32[]{:S(2)}, u32[]{:S(2)}) collective-permute-start(bf16[1024,256]{1,0:T(8,128)(2,1)S(1)} %constant_dynamic-update-slice_fusion.after.refs_5_), channel_id=1, source_target_pairs={{0,8},{8,0},{16,24},{24,16},{32,40},{40,32},{48,56},{56,48},{64,72... | collective-permute-start | bytes 1572872 | tf_op jit(solution)/shard_map/ppermute | solution.py:88
  35.2 2.2 %copy-start = (bf16[1,1,128,128,128]{4,3,2,1,0:T(8,128)(2,1)S(1)}, bf16[1,1,128,128,128]{4,3,2,1,0:T(8,128)(2,1)}, u32[]{:S(2)}) copy-start(bf16[1,1,128,128,128]{4,3,2,1,0:T(8,128)(2,1)} %param.11) | copy-start | bytes 12582916
  37.7 2.0 collective-permute-start.7
  37.8 2.6 %collective-permute-start.8 = (bf16[1024,256]{1,0:T(8,128)(2,1)S(1)}, bf16[1024,256]{1,0:T(8,128)(2,1)S(1)}, u32[]{:S(2)}, u32[]{:S(2)}) collective-permute-start(bf16[1024,256]{1,0:T(8,128)(2,1)S(1)} %collective-permute-done.5.refs_7_), channel_id=1, source_target_pairs={{0,8},{8,0},{16,24},{24,16},{32,40},{40,32},{48,56},{56,48},{64,72... | collective-permute-start | bytes 1572872 | tf_op jit(solution)/shard_map/ppermute | solution.py:88
  38.3 2.9 %collective-permute-start.9 = (bf16[1024,256]{1,0:T(8,128)(2,1)S(1)}, bf16[1024,256]{1,0:T(8,128)(2,1)S(1)}, u32[]{:S(2)}, u32[]{:S(2)}) collective-permute-start(bf16[1024,256]{1,0:T(8,128)(2,1)S(1)} %collective-permute-done.3.refs_11_), channel_id=1, source_target_pairs={{0,8},{8,0},{16,24},{24,16},{32,40},{40,32},{48,56},{56,48},{64,72... | collective-permute-start | bytes 1572872 | tf_op jit(solution)/shard_map/ppermute | solution.py:88
  43.3 12.8 %collective-permute-start.10 = (bf16[256,384]{1,0:T(8,128)(2,1)S(1)}, bf16[256,384]{1,0:T(8,128)(2,1)S(1)}, u32[]{:S(2)}, u32[]{:S(2)}) collective-permute-start(bf16[256,384]{1,0:T(8,128)(2,1)S(1)} %get-tuple-element.98), channel_id=1, source_target_pairs={{0,2},{1,3},{2,4},{3,5},{4,6},{5,7},{6,0},{7,1},{8,10},{9,11},{10,... | collective-permute-start | bytes 589832 | tf_op jit(solution)/shard_map/ppermute | solution.py:123
  46.6 13.3 %collective-permute-start.12 = (bf16[256,384]{1,0:T(8,128)(2,1)S(1)}, bf16[256,384]{1,0:T(8,128)(2,1)S(1)}, u32[]{:S(2)}, u32[]{:S(2)}) collective-permute-start(bf16[256,384]{1,0:T(8,128)(2,1)S(1)} %get-tuple-element.100), channel_id=1, source_target_pairs={{0,6},{1,7},{2,0},{3,1},{4,2},{5,3},{6,4},{7,5},{8,14},{9,15},{10,... | collective-permute-start | bytes 589832 | tf_op jit(solution)/shard_map/ppermute | solution.py:123
  51.5 19.7 %copy-start.1 = (bf16[256,256]{1,0:T(8,128)(2,1)S(1)}, bf16[256,256]{1,0:T(8,128)(2,1)}, u32[]{:S(2)}) copy-start(bf16[256,256]{1,0:T(8,128)(2,1)} %refs_5_.1) | copy-start | bytes 393220
  51.6 19.7 %copy-start.2 = (bf16[256,172]{0,1:T(8,128)(2,1)S(1)}, bf16[256,172]{0,1:T(8,128)(2,1)}, u32[]{:S(2)}) copy-start(bf16[256,172]{0,1:T(8,128)(2,1)} %param.10) | copy-start | bytes 264196
  56.1 9.0 %collective-permute-start.11 = (bf16[256,256]{1,0:T(8,128)(2,1)S(1)}, bf16[256,256]{1,0:T(8,128)(2,1)S(1)}, u32[]{:S(2)}, u32[]{:S(2)}) collective-permute-start(bf16[256,256]{1,0:T(8,128)(2,1)S(1)} %add_convert_fusion.3), channel_id=1, source_target_pairs={{0,2},{1,3},{2,4},{3,5},{4,6},{5,7},{6,0},{7,1},{8,10},{9,11},{10,... | collective-permute-start | bytes 393224 | tf_op jit(solution)/shard_map/ppermute | solution.py:123
  60.0 8.8 %collective-permute-start.13 = (bf16[256,256]{1,0:T(8,128)(2,1)S(1)}, bf16[256,256]{1,0:T(8,128)(2,1)S(1)}, u32[]{:S(2)}, u32[]{:S(2)}) collective-permute-start(bf16[256,256]{1,0:T(8,128)(2,1)S(1)} %add_convert_fusion.2), channel_id=1, source_target_pairs={{0,6},{1,7},{2,0},{3,1},{4,2},{5,3},{6,4},{7,5},{8,14},{9,15},{10,... | collective-permute-start | bytes 393224 | tf_op jit(solution)/shard_map/ppermute | solution.py:123
  62.0 6.8 %collective-permute-start.14 = (bf16[256,256]{1,0:T(8,128)(2,1)S(1)}, bf16[256,256]{1,0:T(8,128)(2,1)S(1)}, u32[]{:S(2)}, u32[]{:S(2)}) collective-permute-start(bf16[256,256]{1,0:T(8,128)(2,1)S(1)} %add_convert_fusion.1), channel_id=1, source_target_pairs={{0,1},{1,2},{2,3},{3,4},{4,5},{5,6},{6,7},{7,0},{8,9},{9,10},{10,1... | collective-permute-start | bytes 393224 | tf_op jit(solution)/shard_map/ppermute | solution.py:123
  62.9 8.4 %collective-permute-start.15 = (bf16[256,256]{1,0:T(8,128)(2,1)S(1)}, bf16[256,256]{1,0:T(8,128)(2,1)S(1)}, u32[]{:S(2)}, u32[]{:S(2)}) collective-permute-start(bf16[256,256]{1,0:T(8,128)(2,1)S(1)} %add_convert_fusion), channel_id=1, source_target_pairs={{0,7},{1,0},{2,1},{3,2},{4,3},{5,4},{6,5},{7,6},{8,15},{9,8},{10,9... | collective-permute-start | bytes 393224 | tf_op jit(solution)/shard_map/ppermute | solution.py:123
  71.5 7.6 %collective-permute-start.16 = (bf16[256,256]{1,0:T(8,128)(2,1)S(1)}, bf16[256,256]{1,0:T(8,128)(2,1)S(1)}, u32[]{:S(2)}, u32[]{:S(2)}) collective-permute-start(bf16[256,256]{1,0:T(8,128)(2,1)S(1)} %get-tuple-element.105), channel_id=1, source_target_pairs={{0,48},{8,200},{16,0},{24,216},{32,16},{40,232},{48,32},{56,248},{... | collective-permute-start | bytes 393224 | tf_op jit(solution)/shard_map/ppermute | solution.py:88
  75.8 5.4 %collective-permute-start.17 = (bf16[256,256]{1,0:T(8,128)(2,1)S(1)}, bf16[256,256]{1,0:T(8,128)(2,1)S(1)}, u32[]{:S(2)}, u32[]{:S(2)}) collective-permute-start(bf16[256,256]{1,0:T(8,128)(2,1)S(1)} %get-tuple-element.105), channel_id=1, source_target_pairs={{0,32},{8,136},{16,48},{24,152},{32,0},{40,168},{48,16},{56,184},{... | collective-permute-start | bytes 393224 | tf_op jit(solution)/shard_map/ppermute | solution.py:88
  75.8 6.5 %collective-permute-start.18 = (bf16[256,256]{1,0:T(8,128)(2,1)S(1)}, bf16[256,256]{1,0:T(8,128)(2,1)S(1)}, u32[]{:S(2)}, u32[]{:S(2)}) collective-permute-start(bf16[256,256]{1,0:T(8,128)(2,1)S(1)} %get-tuple-element.105), channel_id=1, source_target_pairs={{0,16},{8,72},{16,32},{24,88},{32,48},{40,104},{48,0},{56,120},{64... | collective-permute-start | bytes 393224 | tf_op jit(solution)/shard_map/ppermute | solution.py:88
  82.3 8.4 %collective-permute-start.20 = (bf16[1024,256]{1,0:T(8,128)(2,1)S(1)}, bf16[1024,256]{1,0:T(8,128)(2,1)S(1)}, u32[]{:S(2)}, u32[]{:S(2)}) collective-permute-start(bf16[1024,256]{1,0:T(8,128)(2,1)S(1)} %constant_dynamic-update-slice_fusion.4.rest_0_), channel_id=1, source_target_pairs={{0,192},{8,56},{16,208},{24,8},{32,224},{40,24},{48,240},{56,40},{... | collective-permute-start | bytes 1572872 | tf_op jit(solution)/shard_map/ppermute | solution.py:88
  83.0 15.7 %collective-permute-start.21 = (bf16[1024,256]{1,0:T(8,128)(2,1)S(1)}, bf16[1024,256]{1,0:T(8,128)(2,1)S(1)}, u32[]{:S(2)}, u32[]{:S(2)}) collective-permute-start(bf16[1024,256]{1,0:T(8,128)(2,1)S(1)} %constant_dynamic-update-slice_fusion.4.rest_0_), channel_id=1, source_target_pairs={{0,64},{8,24},{16,80},{24,40},{32,96},{40,56},{48,112},{56,8},{64,... | collective-permute-start | bytes 1572872 | tf_op jit(solution)/shard_map/ppermute | solution.py:88
  83.9 17.3 %collective-permute-start.19 = (bf16[1024,256]{1,0:T(8,128)(2,1)S(1)}, bf16[1024,256]{1,0:T(8,128)(2,1)S(1)}, u32[]{:S(2)}, u32[]{:S(2)}) collective-permute-start(bf16[1024,256]{1,0:T(8,128)(2,1)S(1)} %constant_dynamic-update-slice_fusion.4.rest_0_), channel_id=1, source_target_pairs={{0,128},{8,40},{16,144},{24,56},{32,160},{40,8},{48,176},{56,24},{... | collective-permute-start | bytes 1572872 | tf_op jit(solution)/shard_map/ppermute | solution.py:88
  90.7 14.4 %collective-permute-start.22 = (bf16[1024,256]{1,0:T(8,128)(2,1)S(1)}, bf16[1024,256]{1,0:T(8,128)(2,1)S(1)}, u32[]{:S(2)}, u32[]{:S(2)}) collective-permute-start(bf16[1024,256]{1,0:T(8,128)(2,1)S(1)} %constant_dynamic-update-slice_fusion.4.rest_0_), channel_id=1, source_target_pairs={{0,8},{8,0},{16,24},{24,16},{32,40},{40,32},{48,56},{56,48},{64,72... | collective-permute-start | bytes 1572872 | tf_op jit(solution)/shard_map/ppermute | solution.py:88
  98.7 6.4 %collective-permute-start.23 = (bf16[1024,256]{1,0:T(8,128)(2,1)S(1)}, bf16[1024,256]{1,0:T(8,128)(2,1)S(1)}, u32[]{:S(2)}, u32[]{:S(2)}) collective-permute-start(bf16[1024,256]{1,0:T(8,128)(2,1)S(1)} %collective-permute-done.20.rest_1_), channel_id=1, source_target_pairs={{0,8},{8,0},{16,24},{24,16},{32,40},{40,32},{48,56},{56,48},{64,72... | collective-permute-start | bytes 1572872 | tf_op jit(solution)/shard_map/ppermute | solution.py:88
  101.2 5.3 %collective-permute-start.24 = (bf16[1024,256]{1,0:T(8,128)(2,1)S(1)}, bf16[1024,256]{1,0:T(8,128)(2,1)S(1)}, u32[]{:S(2)}, u32[]{:S(2)}) collective-permute-start(bf16[1024,256]{1,0:T(8,128)(2,1)S(1)} %collective-permute-done.21.rest_2_), channel_id=1, source_target_pairs={{0,8},{8,0},{16,24},{24,16},{32,40},{40,32},{48,56},{56,48},{64,72... | collective-permute-start | bytes 1572872 | tf_op jit(solution)/shard_map/ppermute | solution.py:88
  105.0 4.0 %collective-permute-start.25 = (bf16[1024,256]{1,0:T(8,128)(2,1)S(1)}, bf16[1024,256]{1,0:T(8,128)(2,1)S(1)}, u32[]{:S(2)}, u32[]{:S(2)}) collective-permute-start(bf16[1024,256]{1,0:T(8,128)(2,1)S(1)} %collective-permute-done.19.refs_9_), channel_id=1, source_target_pairs={{0,8},{8,0},{16,24},{24,16},{32,40},{40,32},{48,56},{56,48},{64,72... | collective-permute-start | bytes 1572872 | tf_op jit(solution)/shard_map/ppermute | solution.py:88
  112.6 10.3 %collective-permute-start.26 = (bf16[176,384]{1,0:T(8,128)(2,1)S(1)}, bf16[176,384]{1,0:T(8,128)(2,1)S(1)}, u32[]{:S(2)}, u32[]{:S(2)}) collective-permute-start(bf16[176,384]{1,0:T(8,128)(2,1)S(1)} %get-tuple-element.118), channel_id=1, source_target_pairs={{0,2},{1,3},{2,4},{3,5},{4,6},{5,7},{6,0},{7,1},{8,10},{9,11},{10,... | collective-permute-start | bytes 405512 | tf_op jit(solution)/shard_map/ppermute | solution.py:123
  114.1 9.3 %collective-permute-start.28 = (bf16[176,384]{1,0:T(8,128)(2,1)S(1)}, bf16[176,384]{1,0:T(8,128)(2,1)S(1)}, u32[]{:S(2)}, u32[]{:S(2)}) collective-permute-start(bf16[176,384]{1,0:T(8,128)(2,1)S(1)} %get-tuple-element.120), channel_id=1, source_target_pairs={{0,6},{1,7},{2,0},{3,1},{4,2},{5,3},{6,4},{7,5},{8,14},{9,15},{10,... | collective-permute-start | bytes 405512 | tf_op jit(solution)/shard_map/ppermute | solution.py:123
  116.3 15.4 %copy-start.3 = (s32[2048]{0:T(1024)S(1)}, s32[2048]{0:T(1024)}, u32[]{:S(2)}) copy-start(s32[2048]{0:T(1024)} %param.15) | copy-start | bytes 24580
  123.0 6.9 %collective-permute-start.27 = (bf16[176,256]{1,0:T(8,128)(2,1)S(1)}, bf16[176,256]{1,0:T(8,128)(2,1)S(1)}, u32[]{:S(2)}, u32[]{:S(2)}) collective-permute-start(bf16[176,256]{1,0:T(8,128)(2,1)S(1)} %add_convert_fusion.7), channel_id=1, source_target_pairs={{0,2},{1,3},{2,4},{3,5},{4,6},{5,7},{6,0},{7,1},{8,10},{9,11},{10,... | collective-permute-start | bytes 270344 | tf_op jit(solution)/shard_map/ppermute | solution.py:123
  123.5 6.3 %collective-permute-start.29 = (bf16[176,256]{1,0:T(8,128)(2,1)S(1)}, bf16[176,256]{1,0:T(8,128)(2,1)S(1)}, u32[]{:S(2)}, u32[]{:S(2)}) collective-permute-start(bf16[176,256]{1,0:T(8,128)(2,1)S(1)} %add_convert_fusion.6), channel_id=1, source_target_pairs={{0,6},{1,7},{2,0},{3,1},{4,2},{5,3},{6,4},{7,5},{8,14},{9,15},{10,... | collective-permute-start | bytes 270344 | tf_op jit(solution)/shard_map/ppermute | solution.py:123
  127.0 4.7 %collective-permute-start.30 = (bf16[176,256]{1,0:T(8,128)(2,1)S(1)}, bf16[176,256]{1,0:T(8,128)(2,1)S(1)}, u32[]{:S(2)}, u32[]{:S(2)}) collective-permute-start(bf16[176,256]{1,0:T(8,128)(2,1)S(1)} %add_convert_fusion.5), channel_id=1, source_target_pairs={{0,1},{1,2},{2,3},{3,4},{4,5},{5,6},{6,7},{7,0},{8,9},{9,10},{10,1... | collective-permute-start | bytes 270344 | tf_op jit(solution)/shard_map/ppermute | solution.py:123
  127.1 4.6 %collective-permute-start.31 = (bf16[176,256]{1,0:T(8,128)(2,1)S(1)}, bf16[176,256]{1,0:T(8,128)(2,1)S(1)}, u32[]{:S(2)}, u32[]{:S(2)}) collective-permute-start(bf16[176,256]{1,0:T(8,128)(2,1)S(1)} %add_convert_fusion.4), channel_id=1, source_target_pairs={{0,7},{1,0},{2,1},{3,2},{4,3},{5,4},{6,5},{7,6},{8,15},{9,8},{10,9... | collective-permute-start | bytes 270344 | tf_op jit(solution)/shard_map/ppermute | solution.py:123
  132.4 5.2 %collective-permute-start.33 = (bf16[176,256]{1,0:T(8,128)(2,1)S(1)}, bf16[176,256]{1,0:T(8,128)(2,1)S(1)}, u32[]{:S(2)}, u32[]{:S(2)}) collective-permute-start(bf16[176,256]{1,0:T(8,128)(2,1)S(1)} %get-tuple-element.131.refs_5_), channel_id=1, source_target_pairs={{0,6},{1,7},{2,0},{3,1},{4,2},{5,3},{6,4},{7,5},{8,14},{9,15},{10,... | collective-permute-start | bytes 270344 | tf_op jit(solution)/shard_map/ppermute | solution.py:123
  135.6 4.4 %collective-permute-start.32 = (bf16[176,256]{1,0:T(8,128)(2,1)S(1)}, bf16[176,256]{1,0:T(8,128)(2,1)S(1)}, u32[]{:S(2)}, u32[]{:S(2)}) collective-permute-start(bf16[176,256]{1,0:T(8,128)(2,1)S(1)} %get-tuple-element.131.refs_5_), channel_id=1, source_target_pairs={{0,7},{1,0},{2,1},{3,2},{4,3},{5,4},{6,5},{7,6},{8,15},{9,8},{10,9... | collective-permute-start | bytes 270344 | tf_op jit(solution)/shard_map/ppermute | solution.py:123
  135.6 6.9 %collective-permute-start.34 = (bf16[176,256]{1,0:T(8,128)(2,1)S(1)}, bf16[176,256]{1,0:T(8,128)(2,1)S(1)}, u32[]{:S(2)}, u32[]{:S(2)}) collective-permute-start(bf16[176,256]{1,0:T(8,128)(2,1)S(1)} %get-tuple-element.131.refs_5_), channel_id=1, source_target_pairs={{0,2},{1,3},{2,4},{3,5},{4,6},{5,7},{6,0},{7,1},{8,10},{9,11},{10,... | collective-permute-start | bytes 270344 | tf_op jit(solution)/shard_map/ppermute | solution.py:123
  137.5 5.6 %collective-permute-start.35 = (bf16[176,256]{1,0:T(8,128)(2,1)S(1)}, bf16[176,256]{1,0:T(8,128)(2,1)S(1)}, u32[]{:S(2)}, u32[]{:S(2)}) collective-permute-start(bf16[176,256]{1,0:T(8,128)(2,1)S(1)} %get-tuple-element.131.refs_5_), channel_id=1, source_target_pairs={{0,1},{1,2},{2,3},{3,4},{4,5},{5,6},{6,7},{7,0},{8,9},{9,10},{10,1... | collective-permute-start | bytes 270344 | tf_op jit(solution)/shard_map/ppermute | solution.py:123
  140.1 7.1 %collective-permute-start.36 = (bf16[176,384]{1,0:T(8,128)(2,1)S(1)}, bf16[176,384]{1,0:T(8,128)(2,1)S(1)}, u32[]{:S(2)}, u32[]{:S(2)}) collective-permute-start(bf16[176,384]{1,0:T(8,128)(2,1)S(1)} %pad_maximum_fusion), channel_id=1, source_target_pairs={{0,6},{1,7},{2,0},{3,1},{4,2},{5,3},{6,4},{7,5},{8,14},{9,15},{10,... | collective-permute-start | bytes 405512 | tf_op jit(solution)/shard_map/ppermute | solution.py:123
  143.1 8.2 %collective-permute-start.37 = (bf16[176,384]{1,0:T(8,128)(2,1)S(1)}, bf16[176,384]{1,0:T(8,128)(2,1)S(1)}, u32[]{:S(2)}, u32[]{:S(2)}) collective-permute-start(bf16[176,384]{1,0:T(8,128)(2,1)S(1)} %pad_maximum_fusion.1), channel_id=1, source_target_pairs={{0,2},{1,3},{2,4},{3,5},{4,6},{5,7},{6,0},{7,1},{8,10},{9,11},{10,... | collective-permute-start | bytes 405512 | tf_op jit(solution)/shard_map/ppermute | solution.py:123
